TPU v7x, 512 devices: a whole 4x8x8 slice. The times are simulated.
512 devices in a mesh: tm: 128 (over z, y, core), rows: 4 (over x).
Axes of the slice: x: 4, y: 8, z: 8, core: 2. Of those that a mesh axis runs over, the one named last changes fastest.
Arguments:
- phases: bfloat16 [256, 512, 512], P('tm', 'rows'), may hold values from -6 to 6
- focal_data: bfloat16 [256, 2, 256, 256], P('tm', None, 'rows'), may hold values from -6 to 6
- shifts: int32 [256, 2], P('tm'), may hold values from 0 to 2, as said below
- pupil_mask: int32 [512, 512], P('rows'), may hold values 0 or 1
Outputs:
- adjoint_field: float32 [256, 512, 512], P('tm', 'rows')
- wind_grad: float32 [2], replicated
Inputs may be any that keep to these rules, and one draw needn't show every extreme that they name: `shifts`: column 0 is a frame's shift along pupil rows, 0 or 1, and sums over all frames to exactly 32; column 1 is its shift along pupil columns, 0 to 2.
All inputs are finite; a program needn't handle non-finite values. No bound on the sum of `pupil_mask` on one device may be relied on, other than what follows from the above.
Results may differ from a plain program's by a relative error of at most 0.0054.
Values may be sent and summed in bfloat16 or wider, within the bound.
A program may use at most 128 MiB of HBM per device.

v0:
```python
import math

import jax
import jax.numpy as jnp
from jax import lax
from jax.sharding import PartitionSpec as P

PUPIL = 512
FOCAL = 256


decay_rate = 0.999


def from_behind(value, axis, steps):
    count = lax.axis_size(axis)
    first, last = (max(0, -steps), min(count, count - steps))
    return lax.ppermute(value, axis, [(source, source + steps) for source in range(first, last)])


def carried_in(part, axis, combine, identity):
    count = lax.axis_size(axis)
    place = lax.axis_index(axis)
    ahead = count - 1 - place
    gathered = jax.tree.map(lambda a: lax.all_gather(a, axis), part)
    state = jax.tree.map(lambda a, e: jnp.zeros_like(a) + jnp.asarray(e, a.dtype), part, identity)

    def one(step, state):
        source = count - 1 - step
        return combine(
            state, jax.tree.map(lambda a: lax.dynamic_index_in_dim(a, source, 0, False), gathered)
        )

    return lax.fori_loop(0, ahead, one, state)


def tables(row_total):
    focal_pos = jnp.arange(FOCAL, dtype=jnp.int32) - FOCAL // 2
    pupil_pos = jnp.arange(row_total, dtype=jnp.int32) - PUPIL // 2
    turns = jnp.mod(focal_pos[:, None] * pupil_pos[None, :], 2 * PUPIL)
    angle = turns.astype(jnp.float32) * (math.pi / PUPIL)
    factor = 1.0 / math.sqrt(PUPIL)
    return (
        (jnp.cos(angle) * factor).astype(jnp.bfloat16),
        (-jnp.sin(angle) * factor).astype(jnp.bfloat16),
    )


def shift_back(field_in, shift_rows, shift_cols, pad_rows):
    cols_total = field_in.shape[1]
    padded = jnp.pad(field_in, ((0, pad_rows), (0, 0)))
    start_row = jnp.minimum(shift_rows, pad_rows).astype(jnp.int32)
    moved = lax.dynamic_slice(padded, (start_row, jnp.zeros((), jnp.int32)), field_in.shape)
    start_col = jnp.minimum(shift_cols, cols_total).astype(jnp.int32)
    rolled = jnp.roll(moved, -start_col, axis=1)
    keep = jnp.arange(cols_total, dtype=jnp.int32) < cols_total - start_col
    return jnp.where(keep[None, :], rolled, jnp.zeros_like(rolled))


def adjoint_rows(cos_part, sin_part, resid, cos_full, sin_full, live):
    real_part = resid[:, 0]
    imag_part = resid[:, 1]
    w_real = (
        jnp.einsum("qn,kqs->kns", cos_part, real_part, preferred_element_type=jnp.float32)
        + jnp.einsum("qn,kqs->kns", sin_part, imag_part, preferred_element_type=jnp.float32)
    ).astype(jnp.bfloat16)
    w_imag = (
        jnp.einsum("qn,kqs->kns", cos_part, imag_part, preferred_element_type=jnp.float32)
        - jnp.einsum("qn,kqs->kns", sin_part, real_part, preferred_element_type=jnp.float32)
    ).astype(jnp.bfloat16)
    summed = jnp.einsum(
        "kns,sp->knp", w_real, cos_full, preferred_element_type=jnp.float32
    ) + jnp.einsum("kns,sp->knp", w_imag, sin_full, preferred_element_type=jnp.float32)
    return jnp.where(live[None], summed, jnp.zeros_like(summed))


def on_device(phases, focal_data, shifts, pupil_mask):
    frame_count = phases.shape[0]
    block = phases.shape[1]
    width = phases.shape[2]
    halo_rows = width // (4 * lax.axis_size("rows"))
    window = block + halo_rows
    frames_all = frame_count * lax.axis_size("tm")
    row_start = lax.axis_index("rows") * block
    cos_t, sin_t = tables(width)
    cos_rows = lax.dynamic_slice_in_dim(cos_t, row_start, block, 1)
    sin_rows = lax.dynamic_slice_in_dim(sin_t, row_start, block, 1)
    live = pupil_mask == 1
    masked = jnp.where(live[None], phases, jnp.zeros_like(phases))
    y_real = jnp.einsum("kbp,qp->kbq", masked, cos_t, preferred_element_type=jnp.float32).astype(
        jnp.bfloat16
    )
    y_imag = jnp.einsum("kbp,qp->kbq", masked, sin_t, preferred_element_type=jnp.float32).astype(
        jnp.bfloat16
    )
    e_real = jnp.einsum(
        "qb,kbs->kqs", cos_rows, y_real, preferred_element_type=jnp.float32
    ) - jnp.einsum("qb,kbs->kqs", sin_rows, y_imag, preferred_element_type=jnp.float32)
    e_imag = jnp.einsum(
        "qb,kbs->kqs", cos_rows, y_imag, preferred_element_type=jnp.float32
    ) + jnp.einsum("qb,kbs->kqs", sin_rows, y_real, preferred_element_type=jnp.float32)
    partial_field = jnp.stack([e_real, e_imag], axis=1)
    field_share = lax.psum_scatter(partial_field, "rows", scatter_dimension=2, tiled=True)
    resid_share = (focal_data.astype(jnp.float32) - field_share).astype(jnp.bfloat16)
    resid = lax.all_gather(resid_share, "rows", axis=2, tiled=True)
    grad = adjoint_rows(cos_rows, sin_rows, resid, cos_t, sin_t, live)
    outgoing = jnp.concatenate([grad[:, :halo_rows], phases[:, :1].astype(jnp.float32)], axis=1)
    incoming = from_behind(outgoing, "rows", -1)
    grad_window = jnp.concatenate([grad, incoming[:, :halo_rows]], axis=1)
    next_phase = incoming[:, halo_rows]
    lam_next = jnp.zeros((window, width), jnp.float32)
    local_lams = [lam_next] * frame_count
    for frame in reversed(range(frame_count)):
        lam_next = grad_window[frame] + decay_rate * shift_back(
            lam_next, shifts[frame, 0], shifts[frame, 1], halo_rows
        )
        local_lams[frame] = lam_next

    def compose(earlier, later):
        field_late, rows_late, cols_late = earlier
        field_early, rows_early, cols_early = later
        moved = shift_back(field_late, rows_early, cols_early, halo_rows)
        return (field_early + moved, rows_early + rows_late, cols_early + cols_late)

    time_index = lax.axis_index("tm").astype(jnp.float32)
    frames_float = jnp.float32(frame_count)
    start_weight = jnp.power(jnp.float32(decay_rate), time_index * frames_float)
    after_weight = jnp.power(jnp.float32(decay_rate), (time_index + 1.0) * frames_float)
    segment = (start_weight * local_lams[0], jnp.sum(shifts[:, 0]), jnp.sum(shifts[:, 1]))
    identity = (
        jnp.zeros((window, width), jnp.float32),
        jnp.zeros((), jnp.int32),
        jnp.zeros((), jnp.int32),
    )
    carried = carried_in(segment, "tm", compose, identity)
    carry_field = carried[0] / after_weight
    cum_rows = jnp.zeros((), jnp.int32)
    cum_cols = jnp.zeros((), jnp.int32)
    factor_now = 1.0
    results = [None] * frame_count
    wind_terms = jnp.zeros((2,), jnp.float32)
    for frame in reversed(range(frame_count)):
        cum_rows = cum_rows + shifts[frame, 0]
        cum_cols = cum_cols + shifts[frame, 1]
        factor_now = factor_now * decay_rate
        lam_now = (
            local_lams[frame][:block]
            + factor_now * shift_back(carry_field, cum_rows, cum_cols, halo_rows)[:block]
        )
        results[frame] = lam_now
        prior = lam_now - grad[frame]
        phase_wide = phases[frame].astype(jnp.float32)
        down_diff = jnp.concatenate([phase_wide[1:], next_phase[frame][None]], axis=0) - phase_wide
        side_diff = (
            jnp.concatenate([phase_wide[:, 1:], jnp.zeros((block, 1), jnp.float32)], axis=1)
            - phase_wide
        )
        wind_terms = wind_terms + jnp.stack(
            [jnp.sum(prior * down_diff), jnp.sum(prior * side_diff)]
        )
    wind_total = lax.psum(wind_terms, ("tm", "rows"))
    wind_grad = -wind_total / (width * frames_all)
    return (jnp.stack(results), wind_grad)


def solution(mesh):
    in_specs = (P("tm", "rows", None), P("tm", None, "rows", None), P("tm", None), P("rows", None))
    out_specs = (P("tm", "rows", None), P())
    return jax.shard_map(
        on_device, mesh=mesh, in_specs=in_specs, out_specs=out_specs, check_vma=False
    )
```

profile of v0, /device:TPU:1, one launch (start us, length us, event | category | flops | bytes accessed | tf_op | source)
XLA Modules:
  0.0 865.6 jit_solution(9074639214176142363)
XLA Ops:
  8.2 3.2 convolution_convert_fusion
  11.4 3.1 convolution_convert_fusion.1
  14.6 2.5 multiply_convert_fusion
  18.2 1.3 copy.35
  19.6 1.4 fusion.106
  23.5 1.3 dynamic-slice.2
  26.2 54.1 %all-reduce.12.cloned.1.call-done = f32[2,2,256,256]{3,1,0,2:T(2,128)} async-done(((f32[2,2,256,256]{3,1,0,2:T(2,128)}), f32[2,2,256,256]{3,1,0,2:T(2,128)}) %all-reduce.12.cloned.1.call-update) | async-done | bytes 1048592
  82.4 10.7 %all_gather.21 = bf16[2,2,256,256]{3,1,0,2:T(2,128)(2,1)S(1)} all-gather(bf16[2,2,64,256]{3,1,0,2:T(2,128)(2,1)S(1)} %copy.37), channel_id=1, replica_groups=mesh['tm'=128,'rows'=4] {'rows'}, dimensions={2}, use_global_device_ids=true | all-gather | bytes 655360 | tf_op jit(solution)/shard_map/all_gather | solution.py:105
  94.4 2.3 fusion.10
  96.7 2.3 fusion.5
  99.1 1.3 collective-permute-start
  101.8 3.3 collective-permute-done
  109.1 1.3 dynamic-slice
  110.4 1.5 slice_reduce_fusion
  111.9 1.4 dynamic-update-slice.1
  113.3 1.3 dynamic-update-slice
  114.7 27.0 %all-reduce.9 = (s32[128]{0:T(128)S(1)}, s32[128]{0:T(128)S(1)}) all-reduce(s32[128]{0:T(128)S(1)} %dynamic-update-slice, s32[128]{0:T(128)S(1)} %dynamic-update-slice.1), channel_id=1, replica_groups=mesh['tm'=128,'rows'=4] {'tm'}, use_global_device_ids=true, to_apply=%add.6 | all-reduce | flops 256 | bytes 2048
  141.8 132.5 %all-gather.3.cloned.1.call-done = f32[20480,512]{1,0:T(8,128)} async-done(((f32[160,512]{1,0:T(8,128)}), f32[20480,512]{1,0:T(8,128)}) %all-gather.3.cloned.1.call-update) | async-done | bytes 41943056 | tf_op jit(solution)/shard_map/all_gather | solution.py:25
  274.3 482.1 %while.16 = (s32[]{:T(128)}, f32[160,512]{1,0:T(8,128)S(1)}, s32[]{:T(128)}, f32[128,160,512]{2,1,0:T(8,128)}, s32[128]{0:T(128)S(1)}, /*index=5*/s32[128]{0:T(1...) while((s32[]{:T(128)}, f32[160,512]{1,0:T(8,128)S(1)}, ...), condition=%wide.region_4.6_spmd, body=%wide.region_3.5_spmd.sunk | while | flops 246299 | bytes 1639892 | solution.py:34
  299.8 1.2 fusion.112
  303.7 1.2 fusion.112
  307.5 1.2 fusion.112
  757.7 2.6 maximum_add_fusion
  760.3 97.1 %psum.7 = f32[2]{0:T(128)S(1)} all-reduce(f32[2]{0:T(128)S(1)} %maximum_add_fusion), channel_id=1, replica_groups=mesh['tm'=128,'rows'=4] {'tm','rows'}, use_global_device_ids=true, to_apply=%region_9.11 | all-reduce | flops 2 | bytes 16 | tf_op jit(solution)/shard_map/psum | solution.py:161
  (670 shorter events, 317.0 us)
Async XLA Ops:
  7.2 749.4 %copy-start = (bf16[2,128,512]{2,1,0:T(8,128)(2,1)S(1)}, bf16[2,128,512]{2,1,0:T(8,128)(2,1)}, u32[]{:S(2)}) copy-start(bf16[2,128,512]{2,1,0:T(8,128)(2,1)} %param.8) | copy-start | bytes 786436
  7.2 73.1 %all-reduce.12.cloned.1.call-start = ((), (), s32[]{:S(2)}) async-start(), calls=%async_computation.1 | async-start | bytes 2097152
  19.5 254.8 %all-gather.3.cloned.1.call-start = ((), (), s32[]{:S(2)}) async-start(), calls=%async_computation | async-start | bytes 42270720 | tf_op jit(solution)/shard_map/all_gather | solution.py:25
  99.1 6.1 collective-permute-start
Sparse Core Ops, SparseCore 0:
  19.6 60.6 all-reduce.11
  106.6 167.6 all-gather.2
where the time goes:
time: 874 us; the launch traced here: 866 us
  waiting for transfers between devices  190 us (22%)
  loops' own time  173 us (20%)
  other arithmetic  170 us (19%)
  local copies, waits for them, and re-layouts  164 us (19%)
  blocking collectives  135 us (15%)
  between operations  20.1 us (2%)
  matrix products  12.5 us (1%)
    another operation x1, loops' own time, carried_in(): return lax.fori_loop(0, ahead, one, state)  173 us
    add x126, other arithmetic, compose(): return (field_early + moved, rows_early + rows_late, cols_early + cols_late)  155 us
    dynamic_slice x252, local copies, waits for them, and re-layouts, one(): lax.dynamic_index_in_dim(a, source, 0, False)  148 us
    all_gather x1, waiting for transfers between devices, carried_in(): gathered = jax.tree.map(lambda a: lax.all_gather(a, axis), part)  133 us
    psum x1, blocking collectives, on_device(): wind_total = lax.psum(wind_terms, ('tm', 'rows'))  97.1 us
    unnamed x3, waiting for transfers between devices  54.1 us
    unnamed x1, blocking collectives  27 us
  transfers between devices with their start and end apart: 3, of which 3 were waited for; matrix products, arithmetic and copies ran while one was open for 1% of the time, Pallas kernels for 0%

commit v1 on v0

v1 whole, which is shorter than its diff:
```python
import functools
import math

import jax
import jax.numpy as jnp
import numpy as np
from jax import lax
from jax.experimental import pallas as pl
from jax.experimental.pallas import tpu as pltpu
from jax.sharding import PartitionSpec as P

PUPIL = 512
FOCAL = 256
HALO = 32
LANES = 128
DECAY = 0.999
MESH = pl.DeviceIdType.MESH
F32 = jnp.float32
BF16 = jnp.bfloat16


def transform_tables():
    focal_pos = np.arange(FOCAL, dtype=np.int32) - FOCAL // 2
    pupil_pos = np.arange(PUPIL, dtype=np.int32) - PUPIL // 2
    turns = np.mod(focal_pos[:, None] * pupil_pos[None, :], 2 * PUPIL)
    angle = turns.astype(np.float32) * np.float32(math.pi / PUPIL)
    factor = np.float32(1.0 / math.sqrt(PUPIL))
    cos_t = (np.cos(angle) * factor).astype(BF16)
    sin_t = (-np.sin(angle) * factor).astype(BF16)
    half = FOCAL // 2
    by_focal = np.concatenate([cos_t[:half], sin_t[:half], cos_t[half:], sin_t[half:]], axis=0)
    return np.ascontiguousarray(by_focal.T), by_focal


def body(
    Y, Z, X, phases, focal, shifts, mask, by_pupil, by_focal, out, wind,
    y_send, y_recv, f_recv, h_send, h_recv, s_recv, t_recv, resid, w_buf, w_recv,
    grad, gb, bseg, cx, ag, ys, zs, ret, cr, carry, ws, wc, wx, wy, wz,
    y_sem, f_sem, h_sem, s_sem, t_sem, w_sem, c_sem, ys_sem, zs_sem, r_sem, cr_sem,
    wc_sem, wx_sem, wy_sem, wz_sem,
):
    BLOCK = PUPIL // X
    WINDOW = BLOCK + HALO
    PIECES = 2 * Y
    PR = WINDOW * 4 // PIECES
    me = lax.axis_index("tm")
    x = lax.axis_index("rows")
    core = lax.rem(me, 2)
    y = lax.rem(me // 2, Y)
    z = me // (2 * Y)
    other = 1 - core

    def at(x_=None, y_=None, z_=None, c_=None):
        zz = z if z_ is None else z_
        yy = y if y_ is None else y_
        cc = core if c_ is None else c_
        return ((zz * Y + yy) * 2 + cc, x if x_ is None else x_)

    def copy(src, dst, sems, n, device):
        return pltpu.make_async_remote_copy(
            src_ref=src, dst_ref=dst, send_sem=sems.at[0, n], recv_sem=sems.at[1, n],
            device_id=device, device_id_type=MESH,
        )

    def start(copies):
        for c in copies:
            c.start()
        return copies

    def arrive(copies):
        for c in copies:
            c.wait_recv()

    waiting = []

    xs = [lax.rem(x + p, X) for p in range(1, X)]
    yy = [lax.rem(y + p, Y) for p in range(1, Y)]
    zz = [lax.rem(z + p, Z) for p in range(1, Z)]

    barrier = pltpu.get_barrier_semaphore()
    for k in xs:
        pl.semaphore_signal(barrier, inc=1, device_id=at(x_=k), device_id_type=MESH)
    for p in range(1, 2 * Y):
        dev = at(y_=lax.rem(y + p // 2, Y), c_=lax.rem(core + p, 2))
        pl.semaphore_signal(barrier, inc=1, device_id=dev, device_id_type=MESH)
    for k in zz:
        pl.semaphore_signal(barrier, inc=1, device_id=at(z_=k), device_id_type=MESH)

    a0, b0, a1, b1 = shifts[0, 0], shifts[0, 1], shifts[1, 0], shifts[1, 1]
    live = jnp.where(mask[...] == 1, 1.0, 0.0).astype(F32)
    h_send[0:HALO] = live[0:HALO].astype(BF16)
    h_send[HALO : HALO + 16] = phases[0, 0:16]
    h_send[HALO + 16 : HALO + 32] = phases[1, 0:16]
    my_line = y * 2 + core
    s_recv[my_line, 0:8] = jnp.full((8, LANES), a0 + a1, jnp.int32)
    s_recv[my_line, 8:16] = jnp.full((8, LANES), b0 + b1, jnp.int32)
    for f in range(2):
        masked = (phases[f].astype(F32) * live).astype(BF16)
        yv = jnp.dot(masked, by_pupil[...], preferred_element_type=F32).astype(BF16)
        y_send[2 * f] = yv[:, 0:256]
        y_send[2 * f + 1] = yv[:, 256:512]

    pl.semaphore_wait(barrier, (X - 1) + (2 * Y - 1) + (Z - 1))

    rows_of = lambda k: pl.ds(pl.multiple_of(k * BLOCK, BLOCK), BLOCK)
    q_rows = FOCAL // X
    q_of = lambda k: pl.ds(pl.multiple_of(k * q_rows, q_rows), q_rows)
    cols_of = lambda k: pl.ds(pl.multiple_of(lax.rem(k, 2) * LANES, LANES), LANES)

    y_copies = start([
        copy(y_send.at[k], y_recv.at[rows_of(x)], y_sem, n, at(x_=k)) for n, k in enumerate(xs)
    ])
    f_copies = start([
        copy(focal.at[k // 2, :, :, cols_of(k)], f_recv.at[:, q_of(x), :], f_sem, n, at(x_=k))
        for n, k in enumerate(xs)
    ])
    s_copies = start([
        copy(s_recv.at[my_line], s_recv.at[my_line], s_sem, p - 1,
             at(y_=lax.rem(y + p // 2, Y), c_=lax.rem(core + p, 2)))
        for p in range(1, 2 * Y)
    ])
    h_copies = start([copy(h_send, h_recv, h_sem, 0, at(x_=lax.rem(x + X - 1, X)))])
    waiting += y_copies + f_copies + s_copies + h_copies

    y_recv[rows_of(x)] = y_send[x]
    f_recv[:, q_of(x), :] = focal[x // 2, :, :, cols_of(x)]
    w_buf[PUPIL : PUPIL + HALO] = jnp.zeros((HALO, 256), BF16)

    arrive(y_copies)
    m = jnp.dot(by_focal[...], y_recv[...], preferred_element_type=F32)
    arrive(f_copies)
    for h in range(2):
        mc, ms = m[256 * h : 256 * h + 128], m[256 * h + 128 : 256 * h + 256]
        e_real = mc[:, 0:128] - ms[:, 128:256]
        e_imag = mc[:, 128:256] + ms[:, 0:128]
        r_real = (f_recv[0, 128 * h : 128 * h + 128].astype(F32) - e_real).astype(BF16)
        r_imag = (f_recv[1, 128 * h : 128 * h + 128].astype(F32) - e_imag).astype(BF16)
        resid[256 * h : 256 * h + 128, 0:128] = r_real
        resid[256 * h : 256 * h + 128, 128:256] = r_imag
        resid[256 * h + 128 : 256 * h + 256, 0:128] = r_imag
        resid[256 * h + 128 : 256 * h + 256, 128:256] = -r_real
    w_buf[0:PUPIL] = jnp.dot(by_pupil[...], resid[...], preferred_element_type=F32).astype(BF16)
    win_of = lambda k: pl.ds(pl.multiple_of(k * BLOCK, BLOCK), WINDOW)
    w_copies = start([
        copy(w_buf.at[win_of(k)], w_recv.at[x], w_sem, n, at(x_=k)) for n, k in enumerate(xs)
    ])
    waiting += w_copies
    w_recv[x] = w_buf[win_of(x)]

    arrive(s_copies)
    total_shift = s_recv[0]
    for l in range(1, 2 * Y):
        total_shift = total_shift + s_recv[l]
    t_recv[z] = total_shift
    t_copies = start([
        copy(t_recv.at[z], t_recv.at[z], t_sem, n, at(z_=k)) for n, k in enumerate(zz)
    ])
    waiting += t_copies
    arrive(t_copies)
    zero_tile = jnp.zeros((16, LANES), jnp.int32)
    beyond = zero_tile
    z_cols = [None] * Z + [zero_tile[8:9]]
    for k in reversed(range(Z)):
        beyond = beyond + jnp.where(k > z, t_recv[k], zero_tile)
        z_cols[k] = z_cols[k + 1] + t_recv[k, 8:9]
    chip_end = beyond[8:9]
    y_cols = [None] * Y + [chip_end]
    own_sum, c0_sum, c1_sum, c2_sum = beyond, beyond, beyond, beyond
    for k in reversed(range(Y)):
        y_cols[k] = y_cols[k + 1] + s_recv[2 * k + 1, 8:9] + s_recv[2 * k, 8:9]
        for c in range(2):
            line = 2 * k + c
            tile = s_recv[line]
            own_sum = own_sum + jnp.where(line >= my_line, tile, zero_tile)
            c0_sum = c0_sum + jnp.where(line >= 2 * y, tile, zero_tile)
            c1_sum = c1_sum + jnp.where(line >= 2 * y + 1, tile, zero_tile)
            c2_sum = c2_sum + jnp.where(line >= 2 * y + 2, tile, zero_tile)
    row0 = jnp.max(own_sum[0:8])
    row1 = row0 - a0
    col0 = jnp.max(own_sum[8:16])
    col1 = col0 - b0
    col2 = col1 - b1
    chip_col0, chip_col1, chip_col2 = c0_sum[8:9], c1_sum[8:9], c2_sum[8:9]

    lane = lax.broadcasted_iota(jnp.int32, (1, LANES), 1)
    wide = lax.broadcasted_iota(jnp.int32, (1, PUPIL), 1)

    def keep(cols, late, early):
        return jnp.where(((cols - late) & (PUPIL - 1)) >= early - late, 1.0, 0.0).astype(F32)

    def block_cols(piece):
        return lax.rem(piece, 4) * LANES + lane

    arrive(h_copies)
    arrive(w_copies)
    for f in range(2):
        g = jnp.dot(w_recv[2 * f], by_focal[0:256], preferred_element_type=F32) + jnp.dot(
            w_recv[2 * f + 1], by_focal[256:512], preferred_element_type=F32
        )
        grad[f, 0:BLOCK] = g[0:BLOCK] * live
        grad[f, BLOCK:WINDOW] = g[BLOCK:WINDOW] * h_recv[0:HALO].astype(F32)
        turned = pltpu.roll(grad[f], (row0, row1)[f], 0)
        gb[f] = pltpu.roll(turned, (col0, col1)[f] & (PUPIL - 1), 1)
    seg = gb[0] + gb[1] * (DECAY * keep(wide, col1, col0))

    def rows_cols(piece):
        r, c = piece // 4, piece % 4
        return slice(PR * r, PR * r + PR), slice(LANES * c, LANES * c + LANES)

    for m_ in range(PIECES):
        r, c = rows_cols(m_)
        bseg[m_ % 2, m_ // 2] = seg[r, c]

    c_copies = start([
        copy(bseg.at[other], cx.at[other], c_sem, 0, at(c_=other)),
        copy(bseg.at[core], cx.at[core], c_sem, 1, at(c_=other)),
    ])
    waiting += c_copies
    arrive(c_copies[0:1])
    first = core == 0
    for k in range(Y):
        mine, theirs = bseg[core, k], cx[core, k]
        early = jnp.where(first, mine, theirs)
        late = jnp.where(first, theirs, mine)
        ag[k] = early + late * (DECAY**2 * keep(block_cols(2 * k + core), chip_col1, chip_col0))
    ys_copies = start([
        copy(ag.at[k], ys.at[y], ys_sem, n, at(y_=k)) for n, k in enumerate(yy)
    ])
    waiting += ys_copies
    ys[y] = ag[y]
    arrive(ys_copies)
    my_cols = block_cols(my_line)
    later = [None] * Y
    later[Y - 1] = jnp.zeros((PR, LANES), F32)
    for k in reversed(range(Y - 1)):
        later[k] = ys[k + 1] + later[k + 1] * (DECAY**4 * keep(my_cols, y_cols[k + 2], y_cols[k + 1]))
    zs[z] = ys[0] + later[0] * (DECAY**4 * keep(my_cols, y_cols[1], y_cols[0]))
    zs_copies = start([
        copy(zs.at[z], zs.at[z], zs_sem, n, at(z_=k)) for n, k in enumerate(zz)
    ])
    waiting += zs_copies
    arrive(zs_copies)
    acc = jnp.zeros((PR, LANES), F32)
    for k in reversed(range(1, Z)):
        new = zs[k] + acc * (DECAY ** (4 * Y) * keep(my_cols, z_cols[k + 1], z_cols[k]))
        acc = jnp.where(k > z, new, acc)
    for k in range(Y):
        ret[k] = later[k] + acc * (
            DECAY ** (4 * (Y - 1 - k)) * keep(my_cols, chip_end, y_cols[k + 1])
        )
    r_copies = start([
        copy(ret.at[k], cr.at[core, y], r_sem, n, at(y_=k)) for n, k in enumerate(yy)
    ])
    waiting += r_copies
    cr[core, y] = ret[y]
    arrive(r_copies)
    cr_copies = start([copy(cr.at[core], cr.at[core], cr_sem, 0, at(c_=other))])
    waiting += cr_copies
    arrive(c_copies[1:2])
    arrive(cr_copies)
    for m_ in range(PIECES):
        r, c = rows_cols(m_)
        chip = cr[m_ % 2, m_ // 2]
        within = cx[m_ % 2, m_ // 2] + chip * (
            DECAY**2 * keep(block_cols(m_), chip_col2, chip_col1)
        )
        carry[r, c] = jnp.where(first, within, chip)

    tiles = [jnp.zeros((8, LANES), F32), jnp.zeros((8, LANES), F32)]
    inner = jnp.where(x < X - 1, 1.0, 0.0).astype(F32)
    prior_b = carry[...] * (DECAY * keep(wide, col2, col1))
    for f in (1, 0):
        moved = pltpu.roll(prior_b, lax.rem(WINDOW - (row0, row1)[f], WINDOW), 0)[0:BLOCK]
        prior = pltpu.roll(moved, (PUPIL - (col0, col1)[f]) & (PUPIL - 1), 1)
        out[f] = grad[f, 0:BLOCK] + prior
        now = phases[f].astype(F32)
        below = h_recv[HALO + 16 * f : HALO + 16 * f + 16].astype(F32)[0:1] * inner
        down = jnp.concatenate([now[1:], below], axis=0) - now
        side = jnp.where(wide == PUPIL - 1, 0.0, pltpu.roll(now, PUPIL - 1, 1)) - now
        for n, diff in enumerate((down, side)):
            prod = jnp.sum((prior * diff).reshape(BLOCK // 8, 8, PUPIL), axis=0)
            for c in range(4):
                tiles[n] = tiles[n] + prod[:, LANES * c : LANES * c + LANES]
        if f == 1:
            prior_b = (gb[1] + prior_b) * (DECAY * keep(wide, col1, col0))

    def add_up(buf, mine, count, sems, devices):
        value = ws[...]
        buf[mine] = value
        copies = start([
            copy(buf.at[mine], buf.at[mine], sems, n, d) for n, d in enumerate(devices)
        ])
        arrive(copies)
        total = buf[0]
        for k in range(1, count):
            total = total + buf[k]
        ws[...] = total
        return copies

    ws[0:8] = tiles[0]
    ws[8:16] = tiles[1]
    waiting += add_up(wc, core, 2, wc_sem, [at(c_=other)])
    waiting += add_up(wx, x, X, wx_sem, [at(x_=k) for k in xs])
    waiting += add_up(wy, y, Y, wy_sem, [at(y_=k) for k in yy])
    waiting += add_up(wz, z, Z, wz_sem, [at(z_=k) for k in zz])
    scale = -1.0 / (PUPIL * 2.0 * 2 * Y * Z)
    wind[0] = jnp.sum(ws[0:8]) * scale
    wind[1] = jnp.sum(ws[8:16]) * scale
    for c in waiting:
        c.wait_send()


def on_device(Y, Z, X, phases, focal, shifts, mask):
    BLOCK = PUPIL // X
    WINDOW = BLOCK + HALO
    PIECES = 2 * Y
    PR = WINDOW * 4 // PIECES
    by_pupil, by_focal = transform_tables()
    vmem = pl.BlockSpec(memory_space=pltpu.VMEM)
    smem = pl.BlockSpec(memory_space=pltpu.SMEM)
    V = pltpu.VMEM

    def sems(n):
        return pltpu.SemaphoreType.DMA((2, n))

    scratch = [
        V((4, BLOCK, 256), BF16),
        V((PUPIL, 256), BF16),
        V((2, FOCAL, LANES), BF16),
        V((HALO + 32, PUPIL), BF16),
        V((HALO + 32, PUPIL), BF16),
        V((2 * Y, 16, LANES), jnp.int32),
        V((Z, 16, LANES), jnp.int32),
        V((PUPIL, 256), BF16),
        V((PUPIL + HALO, 256), BF16),
        V((X, WINDOW, 256), BF16),
        V((2, WINDOW, PUPIL), F32),
        V((2, WINDOW, PUPIL), F32),
        V((2, Y, PR, LANES), F32),
        V((2, Y, PR, LANES), F32),
        V((Y, PR, LANES), F32),
        V((Y, PR, LANES), F32),
        V((Z, PR, LANES), F32),
        V((Y, PR, LANES), F32),
        V((2, Y, PR, LANES), F32),
        V((WINDOW, PUPIL), F32),
        V((16, LANES), F32),
        V((2, 16, LANES), F32),
        V((X, 16, LANES), F32),
        V((Y, 16, LANES), F32),
        V((Z, 16, LANES), F32),
        sems(X), sems(X), sems(1), sems(2 * Y), sems(Z), sems(X), sems(2), sems(Y), sems(Z), sems(Y),
        sems(1), sems(1), sems(X), sems(Y), sems(Z),
    ]
    return pl.pallas_call(
        functools.partial(body, Y, Z, X),
        name="adjoint_sweep",
        out_shape=(
            jax.ShapeDtypeStruct((2, BLOCK, PUPIL), F32),
            jax.ShapeDtypeStruct((2,), F32),
        ),
        in_specs=[vmem, vmem, smem, vmem, vmem, vmem],
        out_specs=(vmem, smem),
        scratch_shapes=scratch,
        compiler_params=pltpu.CompilerParams(
            collective_id=1, has_side_effects=True, vmem_limit_bytes=40 << 20
        ),
    )(phases, focal, shifts, mask, jnp.asarray(by_pupil), jnp.asarray(by_focal))


def solution(mesh):
    X = mesh.shape["rows"]
    count = mesh.shape["tm"]
    Y = 8 if count == 128 else 2
    Z = count // (2 * Y)
    in_specs = (P("tm", "rows", None), P("tm", None, "rows", None), P("tm", None), P("rows", None))
    out_specs = (P("tm", "rows", None), P())
    return jax.shard_map(
        functools.partial(on_device, Y, Z, X), mesh=mesh, in_specs=in_specs, out_specs=out_specs,
        check_vma=False,
    )
```

time: 874 us -> 74.9 us (0.09)
  the two profiles are of different devices: /device:TPU:1 before, /device:TPU:2 now
where the time goes in v1:
time: 74.9 us; the launch traced here: 74.6 us
  Pallas kernels  67.1 us (90%)
  local copies, waits for them, and re-layouts  6.87 us (9%)
    pallas_call x1, Pallas kernels, on_device(): pl.pallas_call(functools.partial(body, Y, Z, X), name='adjoint_sweep', ou...  67.1 us
    unnamed x14, local copies, waits for them, and re-layouts  6.87 us

profile of v1, /device:TPU:2, one launch (start us, length us, event | category | flops | bytes accessed | tf_op | source)
XLA Modules:
  0.0 74.6 jit_solution(14009163985238176283)
XLA Ops:
  0.6 0.0 copy-start
  0.6 1.0 %copy-done = bf16[512,512]{1,0:T(8,128)(2,1)S(1)} copy-done((bf16[512,512]{1,0:T(8,128)(2,1)S(1)}, bf16[512,512]{1,0:T(8,128)(2,1)}, u32[]{:S(2)}) %copy-start) | copy-done | bytes 524312
  1.7 0.0 copy-start.1
  1.7 1.0 %copy-done.1 = bf16[512,512]{1,0:T(8,128)(2,1)S(1)} copy-done((bf16[512,512]{1,0:T(8,128)(2,1)S(1)}, bf16[512,512]{1,0:T(8,128)(2,1)}, u32[]{:S(2)}) %copy-start.1) | copy-done | bytes 524312
  2.7 0.0 copy-start.2
  2.7 0.9 %copy-done.2 = bf16[2,128,512]{2,1,0:T(8,128)(2,1)S(1)} copy-done((bf16[2,128,512]{2,1,0:T(8,128)(2,1)S(1)}, bf16[2,128,512]{2,1,0:T(8,128)(2,1)}, u32[]{:S(2)}) %copy-start.2) | copy-done | bytes 262168
  3.7 0.0 copy-start.3
  3.7 0.9 %copy-done.3 = s32[128,512]{1,0:T(8,128)S(1)} copy-done((s32[128,512]{1,0:T(8,128)S(1)}, s32[128,512]{1,0:T(8,128)}, u32[]{:S(2)}) %copy-start.3) | copy-done | bytes 262168
  4.6 0.0 copy-start.4
  4.6 0.9 %copy-done.4 = bf16[2,2,64,256]{3,2,1,0:T(8,128)(2,1)S(1)} copy-done((bf16[2,2,64,256]{3,2,1,0:T(8,128)(2,1)S(1)}, bf16[2,2,64,256]{3,2,1,0:T(8,128)(2,1)}, u32[]{:S(2)}) %copy-start.4) | copy-done | bytes 131096
  5.5 0.0 copy-start.5
  5.5 0.7 copy-done.5
  6.2 67.1 %adjoint_sweep.1 = (f32[2,128,512]{2,1,0:T(8,128)S(1)}, f32[2]{0:T(128)S(1)}) custom-call(bf16[2,128,512]{2,1,0:T(8,128)(2,1)S(1)} %copy-done.2, bf16[2,2,64,256]{3,2,1,0:T(8,128)(2,1)S(1)} %copy-done.4, s32[2,2]{1,0:T(2,128)S(1)} %copy-done.5, s32[128,512]{1,0:T(8,128)S(1)} %copy-done.3, bf16[512,512]{1,0:T(8,128)(2,1)S(1)} %copy-done.1, ...), custom_call_target="tpu_custom_call" | custom-call | tf_op jit(solution)/shard_map/adjoint_sweep/pallas_call | solution.py:355
  73.3 0.8 %copy.10 = f32[2,128,512]{2,1,0:T(8,128)} copy(f32[2,128,512]{2,1,0:T(8,128)S(1)} %get-tuple-element.4) | data formatting | bytes 1048576
  74.1 0.5 copy.11
Async XLA Ops:
  0.6 1.0 %copy-start = (bf16[512,512]{1,0:T(8,128)(2,1)S(1)}, bf16[512,512]{1,0:T(8,128)(2,1)}, u32[]{:S(2)}) copy-start(bf16[512,512]{1,0:T(8,128)(2,1)} %constant.5.clone.by_focal) | copy-start | bytes 1572868
  1.7 1.0 %copy-start.1 = (bf16[512,512]{1,0:T(8,128)(2,1)S(1)}, bf16[512,512]{1,0:T(8,128)(2,1)}, u32[]{:S(2)}) copy-start(bf16[512,512]{1,0:T(8,128)(2,1)} %constant.4.clone.by_pupil) | copy-start | bytes 1572868
  2.7 0.9 %copy-start.2 = (bf16[2,128,512]{2,1,0:T(8,128)(2,1)S(1)}, bf16[2,128,512]{2,1,0:T(8,128)(2,1)}, u32[]{:S(2)}) copy-start(bf16[2,128,512]{2,1,0:T(8,128)(2,1)} %phases.1) | copy-start | bytes 786436
  3.7 0.9 %copy-start.3 = (s32[128,512]{1,0:T(8,128)S(1)}, s32[128,512]{1,0:T(8,128)}, u32[]{:S(2)}) copy-start(s32[128,512]{1,0:T(8,128)} %mask.1) | copy-start | bytes 786436
  4.6 0.9 %copy-start.4 = (bf16[2,2,64,256]{3,2,1,0:T(8,128)(2,1)S(1)}, bf16[2,2,64,256]{3,2,1,0:T(8,128)(2,1)}, u32[]{:S(2)}) copy-start(bf16[2,2,64,256]{3,2,1,0:T(8,128)(2,1)} %focal.1) | copy-start | bytes 393220
  5.5 0.7 copy-start.5

commit v2 on v1

--- a/solution.py
+++ b/solution.py
@@ -33,16 +33,18 @@
 
 
 def body(
-    Y, Z, X, phases, focal, shifts, mask, by_pupil, by_focal, out, wind,
+    Y, Z, X, phases_h, focal_h, shifts_h, mask_h, by_pupil_h, by_focal_h, out_h, wind,
+    phases, shifts, mask, by_pupil, by_focal,
     y_send, y_recv, f_recv, h_send, h_recv, s_recv, t_recv, resid, w_buf, w_recv,
-    grad, gb, bseg, cx, ag, ys, zs, ret, cr, carry, ws, wc, wx, wy, wz,
-    y_sem, f_sem, h_sem, s_sem, t_sem, w_sem, c_sem, ys_sem, zs_sem, r_sem, cr_sem,
-    wc_sem, wx_sem, wy_sem, wz_sem,
+    grad, gb, bseg, cx, ag, ys, zs, ret, cr, carry, diffs, d0b, qseg, qx, qc, qy, wz, wy, wx, out,
+    in_sem, out_sem, y_sem, f_sem, h_sem, s_sem, t_sem, w_sem, c_sem, ys_sem, zs_sem, r_sem, cr_sem,
+    qx_sem, qy_sem, wz_sem, wy_sem, wx_sem,
 ):
     BLOCK = PUPIL // X
     WINDOW = BLOCK + HALO
     PIECES = 2 * Y
     PR = WINDOW * 4 // PIECES
+    PR16 = -(-PR // 16) * 16
     me = lax.axis_index("tm")
     x = lax.axis_index("rows")
     core = lax.rem(me, 2)
@@ -77,6 +79,7 @@
     yy = [lax.rem(y + p, Y) for p in range(1, Y)]
     zz = [lax.rem(z + p, Z) for p in range(1, Z)]
 
+    zs[...] = jnp.zeros((Z, PR, LANES), F32)
     barrier = pltpu.get_barrier_semaphore()
     for k in xs:
         pl.semaphore_signal(barrier, inc=1, device_id=at(x_=k), device_id_type=MESH)
@@ -86,6 +89,25 @@
     for k in zz:
         pl.semaphore_signal(barrier, inc=1, device_id=at(z_=k), device_id_type=MESH)
 
+    q_rows = FOCAL // X
+    q_of = lambda k: pl.ds(pl.multiple_of(k * q_rows, q_rows), q_rows)
+    cols_of = lambda k: pl.ds(pl.multiple_of(lax.rem(k, 2) * LANES, LANES), LANES)
+    loads = [
+        pltpu.make_async_copy(src, dst, in_sem.at[n])
+        for n, (src, dst) in enumerate([
+            (shifts_h, shifts),
+            (phases_h, phases),
+            (mask_h, mask),
+            (by_pupil_h, by_pupil),
+            (by_focal_h, by_focal),
+            (focal_h.at[x // 2, :, :, cols_of(x)], f_recv.at[:, q_of(x), :]),
+        ])
+    ]
+    for load in loads:
+        load.start()
+
+    for load in loads[0:3]:
+        load.wait()
     a0, b0, a1, b1 = shifts[0, 0], shifts[0, 1], shifts[1, 0], shifts[1, 1]
     live = jnp.where(mask[...] == 1, 1.0, 0.0).astype(F32)
     h_send[0:HALO] = live[0:HALO].astype(BF16)
@@ -94,6 +116,7 @@
     my_line = y * 2 + core
     s_recv[my_line, 0:8] = jnp.full((8, LANES), a0 + a1, jnp.int32)
     s_recv[my_line, 8:16] = jnp.full((8, LANES), b0 + b1, jnp.int32)
+    loads[3].wait()
     for f in range(2):
         masked = (phases[f].astype(F32) * live).astype(BF16)
         yv = jnp.dot(masked, by_pupil[...], preferred_element_type=F32).astype(BF16)
@@ -103,31 +126,39 @@
     pl.semaphore_wait(barrier, (X - 1) + (2 * Y - 1) + (Z - 1))
 
     rows_of = lambda k: pl.ds(pl.multiple_of(k * BLOCK, BLOCK), BLOCK)
-    q_rows = FOCAL // X
-    q_of = lambda k: pl.ds(pl.multiple_of(k * q_rows, q_rows), q_rows)
-    cols_of = lambda k: pl.ds(pl.multiple_of(lax.rem(k, 2) * LANES, LANES), LANES)
-
     y_copies = start([
         copy(y_send.at[k], y_recv.at[rows_of(x)], y_sem, n, at(x_=k)) for n, k in enumerate(xs)
-    ])
-    f_copies = start([
-        copy(focal.at[k // 2, :, :, cols_of(k)], f_recv.at[:, q_of(x), :], f_sem, n, at(x_=k))
-        for n, k in enumerate(xs)
     ])
     s_copies = start([
         copy(s_recv.at[my_line], s_recv.at[my_line], s_sem, p - 1,
              at(y_=lax.rem(y + p // 2, Y), c_=lax.rem(core + p, 2)))
         for p in range(1, 2 * Y)
     ])
+    f_copies = start([
+        copy(focal_h.at[k // 2, :, :, cols_of(k)], f_recv.at[:, q_of(x), :], f_sem, n, at(x_=k))
+        for n, k in enumerate(xs)
+    ])
     h_copies = start([copy(h_send, h_recv, h_sem, 0, at(x_=lax.rem(x + X - 1, X)))])
     waiting += y_copies + f_copies + s_copies + h_copies
 
     y_recv[rows_of(x)] = y_send[x]
-    f_recv[:, q_of(x), :] = focal[x // 2, :, :, cols_of(x)]
     w_buf[PUPIL : PUPIL + HALO] = jnp.zeros((HALO, 256), BF16)
+    if PR16 > PR:
+        ret[:, PR:PR16] = jnp.zeros((Y, PR16 - PR, LANES), BF16)
 
     arrive(y_copies)
+    loads[4].wait()
     m = jnp.dot(by_focal[...], y_recv[...], preferred_element_type=F32)
+    arrive(s_copies)
+    total_shift = s_recv[0]
+    for l in range(1, 2 * Y):
+        total_shift = total_shift + s_recv[l]
+    t_recv[z] = total_shift
+    t_copies = start([
+        copy(t_recv.at[z], t_recv.at[z], t_sem, n, at(z_=k)) for n, k in enumerate(zz)
+    ])
+    waiting += t_copies
+    loads[5].wait()
     arrive(f_copies)
     for h in range(2):
         mc, ms = m[256 * h : 256 * h + 128], m[256 * h + 128 : 256 * h + 256]
@@ -147,15 +178,18 @@
     waiting += w_copies
     w_recv[x] = w_buf[win_of(x)]
 
-    arrive(s_copies)
-    total_shift = s_recv[0]
-    for l in range(1, 2 * Y):
-        total_shift = total_shift + s_recv[l]
-    t_recv[z] = total_shift
-    t_copies = start([
-        copy(t_recv.at[z], t_recv.at[z], t_sem, n, at(z_=k)) for n, k in enumerate(zz)
-    ])
-    waiting += t_copies
+    lane = lax.broadcasted_iota(jnp.int32, (1, LANES), 1)
+    wide = lax.broadcasted_iota(jnp.int32, (1, PUPIL), 1)
+
+    arrive(h_copies)
+    inner = jnp.where(x < X - 1, 1.0, 0.0).astype(F32)
+    for f in range(2):
+        now = phases[f].astype(F32)
+        below = h_recv[HALO + 16 * f : HALO + 16 * f + 16].astype(F32)[0:1] * inner
+        diffs[f, 0, 0:BLOCK] = jnp.concatenate([now[1:], below], axis=0) - now
+        diffs[f, 1, 0:BLOCK] = jnp.where(wide == PUPIL - 1, 0.0, pltpu.roll(now, PUPIL - 1, 1)) - now
+        for n in range(2):
+            diffs[f, n, BLOCK:WINDOW] = jnp.zeros((HALO, PUPIL), F32)
     arrive(t_copies)
     zero_tile = jnp.zeros((16, LANES), jnp.int32)
     beyond = zero_tile
@@ -182,16 +216,38 @@
     col2 = col1 - b1
     chip_col0, chip_col1, chip_col2 = c0_sum[8:9], c1_sum[8:9], c2_sum[8:9]
 
-    lane = lax.broadcasted_iota(jnp.int32, (1, LANES), 1)
-    wide = lax.broadcasted_iota(jnp.int32, (1, PUPIL), 1)
-
     def keep(cols, late, early):
         return jnp.where(((cols - late) & (PUPIL - 1)) >= early - late, 1.0, 0.0).astype(F32)
 
     def block_cols(piece):
         return lax.rem(piece, 4) * LANES + lane
 
-    arrive(h_copies)
+    def rows_cols(piece):
+        r, c = piece // 4, piece % 4
+        return slice(PR * r, PR * r + PR), slice(LANES * c, LANES * c + LANES)
+
+    def shifted(value, f):
+        turned = pltpu.roll(value, (row0, row1)[f], 0)
+        return pltpu.roll(turned, (col0, col1)[f] & (PUPIL - 1), 1)
+
+    def folded(value):
+        parts = jnp.sum(value.reshape(value.shape[0] // 8, 8, value.shape[1]), axis=0)
+        total = parts[:, 0:LANES]
+        for c in range(1, value.shape[1] // LANES):
+            total = total + parts[:, LANES * c : LANES * c + LANES]
+        return total
+
+    keep_01 = DECAY * keep(wide, col1, col0)
+    keep_12 = DECAY * keep(wide, col2, col1)
+    for n in range(2):
+        d0b[n] = keep_01 * shifted(diffs[0, n], 0)
+        weight = keep_12 * (shifted(diffs[1, n], 1) + d0b[n])
+        for m_ in range(PIECES):
+            r, c = rows_cols(m_)
+            qseg[m_ % 2, m_ // 2, n] = weight[r, c]
+    qx_copies = start([copy(qseg.at[other], qx, qx_sem, 0, at(c_=other))])
+    waiting += qx_copies
+
     arrive(w_copies)
     for f in range(2):
         g = jnp.dot(w_recv[2 * f], by_focal[0:256], preferred_element_type=F32) + jnp.dot(
@@ -199,13 +255,8 @@
         )
         grad[f, 0:BLOCK] = g[0:BLOCK] * live
         grad[f, BLOCK:WINDOW] = g[BLOCK:WINDOW] * h_recv[0:HALO].astype(F32)
-        turned = pltpu.roll(grad[f], (row0, row1)[f], 0)
-        gb[f] = pltpu.roll(turned, (col0, col1)[f] & (PUPIL - 1), 1)
-    seg = gb[0] + gb[1] * (DECAY * keep(wide, col1, col0))
-
-    def rows_cols(piece):
-        r, c = piece // 4, piece % 4
-        return slice(PR * r, PR * r + PR), slice(LANES * c, LANES * c + LANES)
+        gb[f] = shifted(grad[f], f)
+    seg = gb[0] + gb[1] * keep_01
 
     for m_ in range(PIECES):
         r, c = rows_cols(m_)
@@ -228,6 +279,22 @@
     ])
     waiting += ys_copies
     ys[y] = ag[y]
+    arrive(qx_copies)
+    tiles = [folded(gb[1] * d0b[n]) for n in range(2)]
+    for k in range(Y):
+        late = jnp.where(first, cx[core, k], bseg[core, k])
+        keep_k = DECAY**2 * keep(block_cols(2 * k + core), chip_col2, chip_col1)
+        for n in range(2):
+            mine, theirs = qseg[core, k, n], qx[k, n]
+            early_q = jnp.where(first, mine, theirs)
+            late_q = jnp.where(first, theirs, mine)
+            tiles[n] = tiles[n] + folded(late * early_q)
+            qc[k, n] = late_q + keep_k * early_q
+    qy_copies = start([
+        copy(qc.at[k], qy.at[y], qy_sem, n, at(y_=k)) for n, k in enumerate(yy)
+    ])
+    waiting += qy_copies
+    qy[y] = qc[y]
     arrive(ys_copies)
     my_cols = block_cols(my_line)
     later = [None] * Y
@@ -235,24 +302,54 @@
     for k in reversed(range(Y - 1)):
         later[k] = ys[k + 1] + later[k + 1] * (DECAY**4 * keep(my_cols, y_cols[k + 2], y_cols[k + 1]))
     zs[z] = ys[0] + later[0] * (DECAY**4 * keep(my_cols, y_cols[1], y_cols[0]))
-    zs_copies = start([
-        copy(zs.at[z], zs.at[z], zs_sem, n, at(z_=k)) for n, k in enumerate(zz)
-    ])
-    waiting += zs_copies
-    arrive(zs_copies)
+    zs_copies = [copy(zs.at[z], zs.at[z], zs_sem, n, at(z_=k)) for n, k in enumerate(zz)]
+    for n, k in enumerate(zz):
+        pl.when(k < z)(zs_copies[n].start)
+    reach = [
+        DECAY ** (4 * (Y - 1 - k)) * keep(my_cols, chip_end, y_cols[k + 1]) for k in range(Y)
+    ]
+    arrive(qy_copies)
+    whole = [jnp.zeros((PR, LANES), F32) for _ in range(2)]
+    for k in range(Y):
+        for n in range(2):
+            tiles[n] = tiles[n] + folded(later[k] * qy[k, n])
+            whole[n] = whole[n] + reach[k] * qy[k, n]
+    for n in range(len(zz)):
+        pl.when(lax.rem(z + Z - 1 - n, Z) > z)(zs_copies[n].wait_recv)
     acc = jnp.zeros((PR, LANES), F32)
     for k in reversed(range(1, Z)):
         new = zs[k] + acc * (DECAY ** (4 * Y) * keep(my_cols, z_cols[k + 1], z_cols[k]))
         acc = jnp.where(k > z, new, acc)
     for k in range(Y):
-        ret[k] = later[k] + acc * (
-            DECAY ** (4 * (Y - 1 - k)) * keep(my_cols, chip_end, y_cols[k + 1])
-        )
+        ret[k, 0:PR] = (later[k] + acc * reach[k]).astype(BF16)
     r_copies = start([
         copy(ret.at[k], cr.at[core, y], r_sem, n, at(y_=k)) for n, k in enumerate(yy)
     ])
     waiting += r_copies
     cr[core, y] = ret[y]
+
+    def send_sums(buf, mine, sems, devices):
+        copies = start([
+            copy(buf.at[mine], buf.at[mine], sems, n, d) for n, d in enumerate(devices)
+        ])
+        waiting.extend(copies)
+        return copies
+
+    def summed(buf, count):
+        total = buf[0]
+        for k in range(1, count):
+            total = total + buf[k]
+        return total
+
+    for n in range(2):
+        wz[z, 8 * n : 8 * n + 8] = tiles[n] + folded(acc * whole[n])
+    wz_copies = send_sums(wz, z, wz_sem, [at(z_=k) for k in zz])
+    arrive(wz_copies)
+    wy[my_line] = summed(wz, Z)
+    wy_copies = send_sums(
+        wy, my_line, wy_sem,
+        [at(y_=lax.rem(y + p // 2, Y), c_=lax.rem(core + p, 2)) for p in range(1, 2 * Y)],
+    )
     arrive(r_copies)
     cr_copies = start([copy(cr.at[core], cr.at[core], cr_sem, 0, at(c_=other))])
     waiting += cr_copies
@@ -260,52 +357,35 @@
     arrive(cr_copies)
     for m_ in range(PIECES):
         r, c = rows_cols(m_)
-        chip = cr[m_ % 2, m_ // 2]
+        chip = cr[m_ % 2, m_ // 2].astype(F32)[0:PR]
         within = cx[m_ % 2, m_ // 2] + chip * (
             DECAY**2 * keep(block_cols(m_), chip_col2, chip_col1)
         )
         carry[r, c] = jnp.where(first, within, chip)
 
-    tiles = [jnp.zeros((8, LANES), F32), jnp.zeros((8, LANES), F32)]
-    inner = jnp.where(x < X - 1, 1.0, 0.0).astype(F32)
-    prior_b = carry[...] * (DECAY * keep(wide, col2, col1))
+    prior_b = carry[...] * keep_12
+    stores = []
     for f in (1, 0):
         moved = pltpu.roll(prior_b, lax.rem(WINDOW - (row0, row1)[f], WINDOW), 0)[0:BLOCK]
         prior = pltpu.roll(moved, (PUPIL - (col0, col1)[f]) & (PUPIL - 1), 1)
         out[f] = grad[f, 0:BLOCK] + prior
-        now = phases[f].astype(F32)
-        below = h_recv[HALO + 16 * f : HALO + 16 * f + 16].astype(F32)[0:1] * inner
-        down = jnp.concatenate([now[1:], below], axis=0) - now
-        side = jnp.where(wide == PUPIL - 1, 0.0, pltpu.roll(now, PUPIL - 1, 1)) - now
-        for n, diff in enumerate((down, side)):
-            prod = jnp.sum((prior * diff).reshape(BLOCK // 8, 8, PUPIL), axis=0)
-            for c in range(4):
-                tiles[n] = tiles[n] + prod[:, LANES * c : LANES * c + LANES]
+        stores.append(pltpu.make_async_copy(out.at[f], out_h.at[f], out_sem.at[f]))
+        stores[-1].start()
         if f == 1:
-            prior_b = (gb[1] + prior_b) * (DECAY * keep(wide, col1, col0))
-
-    def add_up(buf, mine, count, sems, devices):
-        value = ws[...]
-        buf[mine] = value
-        copies = start([
-            copy(buf.at[mine], buf.at[mine], sems, n, d) for n, d in enumerate(devices)
-        ])
-        arrive(copies)
-        total = buf[0]
-        for k in range(1, count):
-            total = total + buf[k]
-        ws[...] = total
-        return copies
-
-    ws[0:8] = tiles[0]
-    ws[8:16] = tiles[1]
-    waiting += add_up(wc, core, 2, wc_sem, [at(c_=other)])
-    waiting += add_up(wx, x, X, wx_sem, [at(x_=k) for k in xs])
-    waiting += add_up(wy, y, Y, wy_sem, [at(y_=k) for k in yy])
-    waiting += add_up(wz, z, Z, wz_sem, [at(z_=k) for k in zz])
+            prior_b = (gb[1] + prior_b) * keep_01
+
+    arrive(wy_copies)
+    wx[x] = summed(wy, 2 * Y)
+    wx_copies = send_sums(wx, x, wx_sem, [at(x_=k) for k in xs])
+    arrive(wx_copies)
+    total = summed(wx, X)
     scale = -1.0 / (PUPIL * 2.0 * 2 * Y * Z)
-    wind[0] = jnp.sum(ws[0:8]) * scale
-    wind[1] = jnp.sum(ws[8:16]) * scale
+    wind[0] = jnp.sum(total[0:8]) * scale
+    wind[1] = jnp.sum(total[8:16]) * scale
+    for n, k in enumerate(zz):
+        pl.when(k < z)(zs_copies[n].wait_send)
+    for store in stores:
+        store.wait()
     for c in waiting:
         c.wait_send()
 
@@ -315,15 +395,21 @@
     WINDOW = BLOCK + HALO
     PIECES = 2 * Y
     PR = WINDOW * 4 // PIECES
+    PR16 = -(-PR // 16) * 16
     by_pupil, by_focal = transform_tables()
-    vmem = pl.BlockSpec(memory_space=pltpu.VMEM)
     smem = pl.BlockSpec(memory_space=pltpu.SMEM)
+    hbm = pl.BlockSpec(memory_space=pltpu.HBM)
     V = pltpu.VMEM
 
     def sems(n):
         return pltpu.SemaphoreType.DMA((2, n))
 
     scratch = [
+        V((2, BLOCK, PUPIL), BF16),
+        pltpu.SMEM((2, 2), jnp.int32),
+        V((BLOCK, PUPIL), jnp.int32),
+        V((PUPIL, PUPIL), BF16),
+        V((PUPIL, PUPIL), BF16),
         V((4, BLOCK, 256), BF16),
         V((PUPIL, 256), BF16),
         V((2, FOCAL, LANES), BF16),
@@ -341,16 +427,23 @@
         V((Y, PR, LANES), F32),
         V((Y, PR, LANES), F32),
         V((Z, PR, LANES), F32),
-        V((Y, PR, LANES), F32),
-        V((2, Y, PR, LANES), F32),
+        V((Y, PR16, LANES), BF16),
+        V((2, Y, PR16, LANES), BF16),
         V((WINDOW, PUPIL), F32),
-        V((16, LANES), F32),
-        V((2, 16, LANES), F32),
+        V((2, 2, WINDOW, PUPIL), F32),
+        V((2, WINDOW, PUPIL), F32),
+        V((2, Y, 2, PR, LANES), F32),
+        V((Y, 2, PR, LANES), F32),
+        V((Y, 2, PR, LANES), F32),
+        V((Y, 2, PR, LANES), F32),
+        V((Z, 16, LANES), F32),
+        V((2 * Y, 16, LANES), F32),
         V((X, 16, LANES), F32),
-        V((Y, 16, LANES), F32),
-        V((Z, 16, LANES), F32),
+        V((2, BLOCK, PUPIL), F32),
+        pltpu.SemaphoreType.DMA((6,)),
+        pltpu.SemaphoreType.DMA((2,)),
         sems(X), sems(X), sems(1), sems(2 * Y), sems(Z), sems(X), sems(2), sems(Y), sems(Z), sems(Y),
-        sems(1), sems(1), sems(X), sems(Y), sems(Z),
+        sems(1), sems(1), sems(Y), sems(Z), sems(2 * Y), sems(X),
     ]
     return pl.pallas_call(
         functools.partial(body, Y, Z, X),
@@ -359,11 +452,11 @@
             jax.ShapeDtypeStruct((2, BLOCK, PUPIL), F32),
             jax.ShapeDtypeStruct((2,), F32),
         ),
-        in_specs=[vmem, vmem, smem, vmem, vmem, vmem],
-        out_specs=(vmem, smem),
+        in_specs=[hbm] * 6,
+        out_specs=(hbm, smem),
         scratch_shapes=scratch,
         compiler_params=pltpu.CompilerParams(
-            collective_id=1, has_side_effects=True, vmem_limit_bytes=40 << 20
+            collective_id=1, has_side_effects=True, vmem_limit_bytes=63 << 20
         ),
     )(phases, focal, shifts, mask, jnp.asarray(by_pupil), jnp.asarray(by_focal))
 

time: 74.9 us -> 63.5 us (0.85)
  the two profiles are of different devices: /device:TPU:2 before, /device:TPU:1 now
where the time goes in v2:
time: 63.5 us; the launch traced here: 63.4 us
  Pallas kernels  60.3 us (95%)
  local copies, waits for them, and re-layouts  2.38 us (4%)
  between operations  0.65 us (1%)
    pallas_call x1, Pallas kernels, on_device(): pl.pallas_call(functools.partial(body, Y, Z, X), name='adjoint_sweep', ou...  60.3 us
    unnamed x4, local copies, waits for them, and re-layouts  2.38 us

profile of v2, /device:TPU:1, one launch (start us, length us, event | category | flops | bytes accessed | tf_op | source)
XLA Modules:
  0.0 63.4 jit_solution(7170352326951170153)
XLA Ops:
  0.6 60.3 %adjoint_sweep.1 = (f32[2,128,512]{2,1,0:T(8,128)}, f32[2]{0:T(128)}) custom-call(bf16[2,128,512]{2,1,0:T(8,128)(2,1)} %phases_h.1, bf16[2,2,64,256]{3,2,1,0:T(8,128)(2,1)} %focal_h.1, s32[2,2]{1,0:T(2,128)} %shifts_h.1, s32[128,512]{1,0:T(8,128)} %mask_h.1, bf16[512,512]{1,0:T(8,128)(2,1)} %constant.4.clone.by_pupil_h, ...), custom_call_target="tpu_custom_call" | custom-call | tf_op jit(solution)/shard_map/adjoint_sweep/pallas_call | solution.py:448
  61.0 0.0 copy-start
  61.0 1.9 %copy.10 = f32[2,128,512]{2,1,0:T(8,128)} copy(f32[2,128,512]{2,1,0:T(8,128)} %get-tuple-element.4) | data formatting | bytes 1048576
  62.8 0.0 copy-done
  62.8 0.5 copy.11
Async XLA Ops:
  61.0 1.9 %copy-start = (f32[2]{0:T(128)S(1)}, f32[2]{0:T(128)}, u32[]{:S(2)}) copy-start(f32[2]{0:T(128)} %get-tuple-element.5) | copy-start | bytes 28

commit v3 on v2

--- a/solution.py
+++ b/solution.py
@@ -75,19 +75,23 @@
 
     waiting = []
 
-    xs = [lax.rem(x + p, X) for p in range(1, X)]
-    yy = [lax.rem(y + p, Y) for p in range(1, Y)]
-    zz = [lax.rem(z + p, Z) for p in range(1, Z)]
+    def far_first(n):
+        return sorted(range(1, n), key=lambda p: -min(p, n - p))
+
+    xs = [lax.rem(x + p, X) for p in far_first(X)]
+    yy = [lax.rem(y + p, Y) for p in far_first(Y)]
+    zz = [lax.rem(z + p, Z) for p in far_first(Z)]
+    lines = [
+        at(y_=lax.rem(y + p, Y), c_=lax.rem(core + q, 2))
+        for p in far_first(Y) for q in range(2)
+    ] + [at(c_=other)]
 
     zs[...] = jnp.zeros((Z, PR, LANES), F32)
     barrier = pltpu.get_barrier_semaphore()
     for k in xs:
         pl.semaphore_signal(barrier, inc=1, device_id=at(x_=k), device_id_type=MESH)
-    for p in range(1, 2 * Y):
-        dev = at(y_=lax.rem(y + p // 2, Y), c_=lax.rem(core + p, 2))
+    for dev in [at(z_=k) for k in zz] + lines:
         pl.semaphore_signal(barrier, inc=1, device_id=dev, device_id_type=MESH)
-    for k in zz:
-        pl.semaphore_signal(barrier, inc=1, device_id=at(z_=k), device_id_type=MESH)
 
     q_rows = FOCAL // X
     q_of = lambda k: pl.ds(pl.multiple_of(k * q_rows, q_rows), q_rows)
@@ -98,7 +102,7 @@
             (shifts_h, shifts),
             (phases_h, phases),
             (mask_h, mask),
-            (by_pupil_h, by_pupil),
+            (by_pupil_h, by_pupil.at[0:PUPIL]),
             (by_focal_h, by_focal),
             (focal_h.at[x // 2, :, :, cols_of(x)], f_recv.at[:, q_of(x), :]),
         ])
@@ -114,12 +118,12 @@
     h_send[HALO : HALO + 16] = phases[0, 0:16]
     h_send[HALO + 16 : HALO + 32] = phases[1, 0:16]
     my_line = y * 2 + core
-    s_recv[my_line, 0:8] = jnp.full((8, LANES), a0 + a1, jnp.int32)
-    s_recv[my_line, 8:16] = jnp.full((8, LANES), b0 + b1, jnp.int32)
+    s_recv[my_line, 0:1] = jnp.full((1, LANES), a0 + a1, jnp.int32)
+    s_recv[my_line, 1:2] = jnp.full((1, LANES), b0 + b1, jnp.int32)
     loads[3].wait()
     for f in range(2):
         masked = (phases[f].astype(F32) * live).astype(BF16)
-        yv = jnp.dot(masked, by_pupil[...], preferred_element_type=F32).astype(BF16)
+        yv = jnp.dot(masked, by_pupil[0:PUPIL], preferred_element_type=F32).astype(BF16)
         y_send[2 * f] = yv[:, 0:256]
         y_send[2 * f + 1] = yv[:, 256:512]
 
@@ -130,9 +134,7 @@
         copy(y_send.at[k], y_recv.at[rows_of(x)], y_sem, n, at(x_=k)) for n, k in enumerate(xs)
     ])
     s_copies = start([
-        copy(s_recv.at[my_line], s_recv.at[my_line], s_sem, p - 1,
-             at(y_=lax.rem(y + p // 2, Y), c_=lax.rem(core + p, 2)))
-        for p in range(1, 2 * Y)
+        copy(s_recv.at[my_line], s_recv.at[my_line], s_sem, n, dev) for n, dev in enumerate(lines)
     ])
     f_copies = start([
         copy(focal_h.at[k // 2, :, :, cols_of(k)], f_recv.at[:, q_of(x), :], f_sem, n, at(x_=k))
@@ -142,7 +144,7 @@
     waiting += y_copies + f_copies + s_copies + h_copies
 
     y_recv[rows_of(x)] = y_send[x]
-    w_buf[PUPIL : PUPIL + HALO] = jnp.zeros((HALO, 256), BF16)
+    by_pupil[PUPIL : PUPIL + HALO] = jnp.zeros((HALO, PUPIL), BF16)
     if PR16 > PR:
         ret[:, PR:PR16] = jnp.zeros((Y, PR16 - PR, LANES), BF16)
 
@@ -170,13 +172,16 @@
         resid[256 * h : 256 * h + 128, 128:256] = r_imag
         resid[256 * h + 128 : 256 * h + 256, 0:128] = r_imag
         resid[256 * h + 128 : 256 * h + 256, 128:256] = -r_real
-    w_buf[0:PUPIL] = jnp.dot(by_pupil[...], resid[...], preferred_element_type=F32).astype(BF16)
     win_of = lambda k: pl.ds(pl.multiple_of(k * BLOCK, BLOCK), WINDOW)
-    w_copies = start([
-        copy(w_buf.at[win_of(k)], w_recv.at[x], w_sem, n, at(x_=k)) for n, k in enumerate(xs)
-    ])
+    w_copies = []
+    for n, k in enumerate(xs + [x]):
+        rows = jnp.dot(by_pupil[win_of(k)], resid[...], preferred_element_type=F32)
+        if n == X - 1:
+            w_recv[x] = rows.astype(BF16)
+        else:
+            w_buf[n] = rows.astype(BF16)
+            w_copies += start([copy(w_buf.at[n], w_recv.at[x], w_sem, n, at(x_=k))])
     waiting += w_copies
-    w_recv[x] = w_buf[win_of(x)]
 
     lane = lax.broadcasted_iota(jnp.int32, (1, LANES), 1)
     wide = lax.broadcasted_iota(jnp.int32, (1, PUPIL), 1)
@@ -191,17 +196,17 @@
         for n in range(2):
             diffs[f, n, BLOCK:WINDOW] = jnp.zeros((HALO, PUPIL), F32)
     arrive(t_copies)
-    zero_tile = jnp.zeros((16, LANES), jnp.int32)
+    zero_tile = jnp.zeros((2, LANES), jnp.int32)
     beyond = zero_tile
-    z_cols = [None] * Z + [zero_tile[8:9]]
+    z_cols = [None] * Z + [zero_tile[1:2]]
     for k in reversed(range(Z)):
         beyond = beyond + jnp.where(k > z, t_recv[k], zero_tile)
-        z_cols[k] = z_cols[k + 1] + t_recv[k, 8:9]
-    chip_end = beyond[8:9]
+        z_cols[k] = z_cols[k + 1] + t_recv[k, 1:2]
+    chip_end = beyond[1:2]
     y_cols = [None] * Y + [chip_end]
     own_sum, c0_sum, c1_sum, c2_sum = beyond, beyond, beyond, beyond
     for k in reversed(range(Y)):
-        y_cols[k] = y_cols[k + 1] + s_recv[2 * k + 1, 8:9] + s_recv[2 * k, 8:9]
+        y_cols[k] = y_cols[k + 1] + s_recv[2 * k + 1, 1:2] + s_recv[2 * k, 1:2]
         for c in range(2):
             line = 2 * k + c
             tile = s_recv[line]
@@ -209,12 +214,12 @@
             c0_sum = c0_sum + jnp.where(line >= 2 * y, tile, zero_tile)
             c1_sum = c1_sum + jnp.where(line >= 2 * y + 1, tile, zero_tile)
             c2_sum = c2_sum + jnp.where(line >= 2 * y + 2, tile, zero_tile)
-    row0 = jnp.max(own_sum[0:8])
+    row0 = jnp.max(own_sum[0:1])
     row1 = row0 - a0
-    col0 = jnp.max(own_sum[8:16])
+    col0 = jnp.max(own_sum[1:2])
     col1 = col0 - b0
     col2 = col1 - b1
-    chip_col0, chip_col1, chip_col2 = c0_sum[8:9], c1_sum[8:9], c2_sum[8:9]
+    chip_col0, chip_col1, chip_col2 = c0_sum[1:2], c1_sum[1:2], c2_sum[1:2]
 
     def keep(cols, late, early):
         return jnp.where(((cols - late) & (PUPIL - 1)) >= early - late, 1.0, 0.0).astype(F32)
@@ -314,8 +319,8 @@
         for n in range(2):
             tiles[n] = tiles[n] + folded(later[k] * qy[k, n])
             whole[n] = whole[n] + reach[k] * qy[k, n]
-    for n in range(len(zz)):
-        pl.when(lax.rem(z + Z - 1 - n, Z) > z)(zs_copies[n].wait_recv)
+    for n, p in enumerate(far_first(Z)):
+        pl.when(lax.rem(z + Z - p, Z) > z)(zs_copies[n].wait_recv)
     acc = jnp.zeros((PR, LANES), F32)
     for k in reversed(range(1, Z)):
         new = zs[k] + acc * (DECAY ** (4 * Y) * keep(my_cols, z_cols[k + 1], z_cols[k]))
@@ -342,14 +347,11 @@
         return total
 
     for n in range(2):
-        wz[z, 8 * n : 8 * n + 8] = tiles[n] + folded(acc * whole[n])
+        wz[z, n : n + 1] = jnp.sum(tiles[n] + folded(acc * whole[n]), axis=0, keepdims=True)
     wz_copies = send_sums(wz, z, wz_sem, [at(z_=k) for k in zz])
     arrive(wz_copies)
     wy[my_line] = summed(wz, Z)
-    wy_copies = send_sums(
-        wy, my_line, wy_sem,
-        [at(y_=lax.rem(y + p // 2, Y), c_=lax.rem(core + p, 2)) for p in range(1, 2 * Y)],
-    )
+    wy_copies = send_sums(wy, my_line, wy_sem, lines)
     arrive(r_copies)
     cr_copies = start([copy(cr.at[core], cr.at[core], cr_sem, 0, at(c_=other))])
     waiting += cr_copies
@@ -380,14 +382,31 @@
     arrive(wx_copies)
     total = summed(wx, X)
     scale = -1.0 / (PUPIL * 2.0 * 2 * Y * Z)
-    wind[0] = jnp.sum(total[0:8]) * scale
-    wind[1] = jnp.sum(total[8:16]) * scale
+    wind[0] = jnp.sum(total[0:1]) * scale
+    wind[1] = jnp.sum(total[1:2]) * scale
     for n, k in enumerate(zz):
         pl.when(k < z)(zs_copies[n].wait_send)
     for store in stores:
         store.wait()
     for c in waiting:
         c.wait_send()
+
+
+def finish(field_h, sums_h, out_h, wind_h, sem):
+    frames = field_h.shape[0]
+    parts = 4
+    rows = field_h.shape[1] // parts
+    copies = [pltpu.make_async_copy(sums_h, wind_h, sem.at[0])]
+    for f in range(frames):
+        for p in range(parts):
+            here = (f, pl.ds(p * rows, rows))
+            copies.append(
+                pltpu.make_async_copy(field_h.at[here], out_h.at[here], sem.at[1 + f * parts + p])
+            )
+    for c in copies:
+        c.start()
+    for c in copies:
+        c.wait()
 
 
 def on_device(Y, Z, X, phases, focal, shifts, mask):
@@ -408,17 +427,17 @@
         V((2, BLOCK, PUPIL), BF16),
         pltpu.SMEM((2, 2), jnp.int32),
         V((BLOCK, PUPIL), jnp.int32),
-        V((PUPIL, PUPIL), BF16),
+        V((PUPIL + HALO, PUPIL), BF16),
         V((PUPIL, PUPIL), BF16),
         V((4, BLOCK, 256), BF16),
         V((PUPIL, 256), BF16),
         V((2, FOCAL, LANES), BF16),
         V((HALO + 32, PUPIL), BF16),
         V((HALO + 32, PUPIL), BF16),
-        V((2 * Y, 16, LANES), jnp.int32),
-        V((Z, 16, LANES), jnp.int32),
+        V((2 * Y, 2, LANES), jnp.int32),
+        V((Z, 2, LANES), jnp.int32),
         V((PUPIL, 256), BF16),
-        V((PUPIL + HALO, 256), BF16),
+        V((X, WINDOW, 256), BF16),
         V((X, WINDOW, 256), BF16),
         V((2, WINDOW, PUPIL), F32),
         V((2, WINDOW, PUPIL), F32),
@@ -436,22 +455,23 @@
         V((Y, 2, PR, LANES), F32),
         V((Y, 2, PR, LANES), F32),
         V((Y, 2, PR, LANES), F32),
-        V((Z, 16, LANES), F32),
-        V((2 * Y, 16, LANES), F32),
-        V((X, 16, LANES), F32),
+        V((Z, 2, LANES), F32),
+        V((2 * Y, 2, LANES), F32),
+        V((X, 2, LANES), F32),
         V((2, BLOCK, PUPIL), F32),
         pltpu.SemaphoreType.DMA((6,)),
         pltpu.SemaphoreType.DMA((2,)),
         sems(X), sems(X), sems(1), sems(2 * Y), sems(Z), sems(X), sems(2), sems(Y), sems(Z), sems(Y),
         sems(1), sems(1), sems(Y), sems(Z), sems(2 * Y), sems(X),
     ]
-    return pl.pallas_call(
+    shapes = (
+        jax.ShapeDtypeStruct((2, BLOCK, PUPIL), F32),
+        jax.ShapeDtypeStruct((2,), F32),
+    )
+    field, sums = pl.pallas_call(
         functools.partial(body, Y, Z, X),
         name="adjoint_sweep",
-        out_shape=(
-            jax.ShapeDtypeStruct((2, BLOCK, PUPIL), F32),
-            jax.ShapeDtypeStruct((2,), F32),
-        ),
+        out_shape=shapes,
         in_specs=[hbm] * 6,
         out_specs=(hbm, smem),
         scratch_shapes=scratch,
@@ -459,6 +479,15 @@
             collective_id=1, has_side_effects=True, vmem_limit_bytes=63 << 20
         ),
     )(phases, focal, shifts, mask, jnp.asarray(by_pupil), jnp.asarray(by_focal))
+    return pl.pallas_call(
+        finish,
+        name="finish",
+        out_shape=shapes,
+        in_specs=[hbm, hbm],
+        out_specs=(hbm, hbm),
+        scratch_shapes=[pltpu.SemaphoreType.DMA((9,))],
+        compiler_params=pltpu.CompilerParams(vmem_limit_bytes=63 << 20),
+    )(field, sums)
 
 
 def solution(mesh):

time: 63.5 us -> 72.9 us (1.15)
  Pallas kernels: 60.3 us -> 72.1 us
  local copies, waits for them, and re-layouts: 2.38 us -> 0 us
    pallas_call x0 -> x1, Pallas kernels: none -> 17.1 us  [on_device(): pl.pallas_call(finish, name='finish', out_shape=shapes, in_specs=[hbm, hb...]
    pallas_call x1, Pallas kernels: 60.3 us -> 55 us  [on_device(): pl.pallas_call(functools.partial(body, Y, Z, X), name='adjoint_sweep', ou...]
    unnamed x4 -> x0, local copies, waits for them, and re-layouts: 2.38 us -> none
where the time goes in v3:
time: 72.9 us; the launch traced here: 72.7 us
  Pallas kernels  72.1 us (99%)
    pallas_call x1, Pallas kernels, on_device(): pl.pallas_call(functools.partial(body, Y, Z, X), name='adjoint_sweep', ou...  55 us
    pallas_call x1, Pallas kernels, on_device(): pl.pallas_call(finish, name='finish', out_shape=shapes, in_specs=[hbm, hb...  17.1 us

profile of v3, /device:TPU:1, one launch (start us, length us, event | category | flops | bytes accessed | tf_op | source)
XLA Modules:
  0.0 72.7 jit_solution(18230330250473862525)
XLA Ops:
  0.6 55.0 %adjoint_sweep.1 = (f32[2,128,512]{2,1,0:T(8,128)}, f32[2]{0:T(128)}) custom-call(bf16[2,128,512]{2,1,0:T(8,128)(2,1)} %phases_h.1, bf16[2,2,64,256]{3,2,1,0:T(8,128)(2,1)} %focal_h.1, s32[2,2]{1,0:T(2,128)} %shifts_h.1, s32[128,512]{1,0:T(8,128)} %mask_h.1, bf16[512,512]{1,0:T(8,128)(2,1)} %constant.4.clone.by_pupil_h, ...), custom_call_target="tpu_custom_call" | custom-call | tf_op jit(solution)/shard_map/adjoint_sweep/pallas_call | solution.py:471
  55.6 17.1 %finish.1 = (f32[2,128,512]{2,1,0:T(8,128)}, f32[2]{0:T(128)}) custom-call(f32[2,128,512]{2,1,0:T(8,128)} %get-tuple-element.4.field_h, f32[2]{0:T(128)} %get-tuple-element.5.sums_h), custom_call_target="tpu_custom_call" | custom-call | tf_op jit(solution)/shard_map/finish/pallas_call | solution.py:482

commit v4 on v3

--- a/solution.py
+++ b/solution.py
@@ -35,10 +35,10 @@
 def body(
     Y, Z, X, phases_h, focal_h, shifts_h, mask_h, by_pupil_h, by_focal_h, out_h, wind,
     phases, shifts, mask, by_pupil, by_focal,
-    y_send, y_recv, f_recv, h_send, h_recv, s_recv, t_recv, resid, w_buf, w_recv,
-    grad, gb, bseg, cx, ag, ys, zs, ret, cr, carry, diffs, d0b, qseg, qx, qc, qy, wz, wy, wx, out,
+    y_send, y_recv, f_recv, h_send, h_recv, p_send, p_recv, s_recv, t_recv, resid, w_buf, w_recv,
+    grad, gb, bseg, cx, ag, ys, zs, ret, cr, carry, diffs, d0b, qseg, qx, qc, qy, wz, wy, out,
     in_sem, out_sem, y_sem, f_sem, h_sem, s_sem, t_sem, w_sem, c_sem, ys_sem, zs_sem, r_sem, cr_sem,
-    qx_sem, qy_sem, wz_sem, wy_sem, wx_sem,
+    qx_sem, qy_sem, wz_sem, wy_sem, sc_sem, ring_sem,
 ):
     BLOCK = PUPIL // X
     WINDOW = BLOCK + HALO
@@ -87,12 +87,23 @@
     ] + [at(c_=other)]
 
     zs[...] = jnp.zeros((Z, PR, LANES), F32)
+    def ring(d):
+        near_y = [at(y_=lax.rem(y + p, Y)) for p in sorted({d % Y, -d % Y})]
+        return near_y + [at(z_=lax.rem(z + p, Z)) for p in sorted({d % Z, -d % Z})]
+
+    rounds = [d for d in (1, 2) if 2 * d < max(Y, Z)]
+
+    def announce(n):
+        for dev in ring(rounds[n]):
+            pl.semaphore_signal(ring_sem.at[n], inc=1, device_id=dev, device_id_type=MESH)
+
+    def heard(n):
+        pl.semaphore_wait(ring_sem.at[n], len(ring(rounds[n])))
+
     barrier = pltpu.get_barrier_semaphore()
-    for k in xs:
-        pl.semaphore_signal(barrier, inc=1, device_id=at(x_=k), device_id_type=MESH)
-    for dev in [at(z_=k) for k in zz] + lines:
+    entry = [at(x_=k) for k in xs] + ring(1) + [at(c_=other)]
+    for dev in entry:
         pl.semaphore_signal(barrier, inc=1, device_id=dev, device_id_type=MESH)
-
     q_rows = FOCAL // X
     q_of = lambda k: pl.ds(pl.multiple_of(k * q_rows, q_rows), q_rows)
     cols_of = lambda k: pl.ds(pl.multiple_of(lax.rem(k, 2) * LANES, LANES), LANES)
@@ -115,11 +126,16 @@
     a0, b0, a1, b1 = shifts[0, 0], shifts[0, 1], shifts[1, 0], shifts[1, 1]
     live = jnp.where(mask[...] == 1, 1.0, 0.0).astype(F32)
     h_send[0:HALO] = live[0:HALO].astype(BF16)
-    h_send[HALO : HALO + 16] = phases[0, 0:16]
-    h_send[HALO + 16 : HALO + 32] = phases[1, 0:16]
+    for f in range(2):
+        p_send[f : f + 1] = phases[f, 0:16].astype(F32)[0:1]
     my_line = y * 2 + core
-    s_recv[my_line, 0:1] = jnp.full((1, LANES), a0 + a1, jnp.int32)
-    s_recv[my_line, 1:2] = jnp.full((1, LANES), b0 + b1, jnp.int32)
+    s_recv[y, core, 0:1] = jnp.full((1, LANES), a0 + a1, jnp.int32)
+    s_recv[y, core, 1:2] = jnp.full((1, LANES), b0 + b1, jnp.int32)
+    pl.semaphore_wait(barrier, len(entry))
+    if rounds:
+        announce(0)
+    sc_copies = start([copy(s_recv.at[y, core], s_recv.at[y, core], sc_sem, 0, at(c_=other))])
+    waiting += sc_copies
     loads[3].wait()
     for f in range(2):
         masked = (phases[f].astype(F32) * live).astype(BF16)
@@ -127,21 +143,29 @@
         y_send[2 * f] = yv[:, 0:256]
         y_send[2 * f + 1] = yv[:, 256:512]
 
-    pl.semaphore_wait(barrier, (X - 1) + (2 * Y - 1) + (Z - 1))
 
     rows_of = lambda k: pl.ds(pl.multiple_of(k * BLOCK, BLOCK), BLOCK)
     y_copies = start([
         copy(y_send.at[k], y_recv.at[rows_of(x)], y_sem, n, at(x_=k)) for n, k in enumerate(xs)
     ])
-    s_copies = start([
-        copy(s_recv.at[my_line], s_recv.at[my_line], s_sem, n, dev) for n, dev in enumerate(lines)
-    ])
     f_copies = start([
         copy(focal_h.at[k // 2, :, :, cols_of(k)], f_recv.at[:, q_of(x), :], f_sem, n, at(x_=k))
         for n, k in enumerate(xs)
     ])
-    h_copies = start([copy(h_send, h_recv, h_sem, 0, at(x_=lax.rem(x + X - 1, X)))])
-    waiting += y_copies + f_copies + s_copies + h_copies
+    above = at(x_=lax.rem(x + X - 1, X))
+    h_copies = start([
+        copy(p_send, p_recv, h_sem, 0, above), copy(h_send, h_recv, h_sem, 1, above)
+    ])
+    waiting += y_copies + f_copies + h_copies
+    for n in range(len(rounds)):
+        heard(n)
+        if n + 1 < len(rounds):
+            announce(n + 1)
+    arrive(sc_copies)
+    s_copies = start([
+        copy(s_recv.at[y], s_recv.at[y], s_sem, n, at(y_=k)) for n, k in enumerate(yy)
+    ])
+    waiting += s_copies
 
     y_recv[rows_of(x)] = y_send[x]
     by_pupil[PUPIL : PUPIL + HALO] = jnp.zeros((HALO, PUPIL), BF16)
@@ -151,15 +175,6 @@
     arrive(y_copies)
     loads[4].wait()
     m = jnp.dot(by_focal[...], y_recv[...], preferred_element_type=F32)
-    arrive(s_copies)
-    total_shift = s_recv[0]
-    for l in range(1, 2 * Y):
-        total_shift = total_shift + s_recv[l]
-    t_recv[z] = total_shift
-    t_copies = start([
-        copy(t_recv.at[z], t_recv.at[z], t_sem, n, at(z_=k)) for n, k in enumerate(zz)
-    ])
-    waiting += t_copies
     loads[5].wait()
     arrive(f_copies)
     for h in range(2):
@@ -183,6 +198,17 @@
             w_copies += start([copy(w_buf.at[n], w_recv.at[x], w_sem, n, at(x_=k))])
     waiting += w_copies
 
+    arrive(s_copies)
+    total_shift = jnp.zeros((2, LANES), jnp.int32)
+    for k in range(Y):
+        for c in range(2):
+            total_shift = total_shift + s_recv[k, c]
+    t_recv[z] = total_shift
+    t_copies = start([
+        copy(t_recv.at[z], t_recv.at[z], t_sem, n, at(z_=k)) for n, k in enumerate(zz)
+    ])
+    waiting += t_copies
+
     lane = lax.broadcasted_iota(jnp.int32, (1, LANES), 1)
     wide = lax.broadcasted_iota(jnp.int32, (1, PUPIL), 1)
 
@@ -190,7 +216,7 @@
     inner = jnp.where(x < X - 1, 1.0, 0.0).astype(F32)
     for f in range(2):
         now = phases[f].astype(F32)
-        below = h_recv[HALO + 16 * f : HALO + 16 * f + 16].astype(F32)[0:1] * inner
+        below = p_recv[f : f + 1] * inner
         diffs[f, 0, 0:BLOCK] = jnp.concatenate([now[1:], below], axis=0) - now
         diffs[f, 1, 0:BLOCK] = jnp.where(wide == PUPIL - 1, 0.0, pltpu.roll(now, PUPIL - 1, 1)) - now
         for n in range(2):
@@ -206,10 +232,10 @@
     y_cols = [None] * Y + [chip_end]
     own_sum, c0_sum, c1_sum, c2_sum = beyond, beyond, beyond, beyond
     for k in reversed(range(Y)):
-        y_cols[k] = y_cols[k + 1] + s_recv[2 * k + 1, 1:2] + s_recv[2 * k, 1:2]
+        y_cols[k] = y_cols[k + 1] + s_recv[k, 1, 1:2] + s_recv[k, 0, 1:2]
         for c in range(2):
             line = 2 * k + c
-            tile = s_recv[line]
+            tile = s_recv[k, c]
             own_sum = own_sum + jnp.where(line >= my_line, tile, zero_tile)
             c0_sum = c0_sum + jnp.where(line >= 2 * y, tile, zero_tile)
             c1_sum = c1_sum + jnp.where(line >= 2 * y + 1, tile, zero_tile)
@@ -333,25 +359,27 @@
     waiting += r_copies
     cr[core, y] = ret[y]
 
-    def send_sums(buf, mine, sems, devices):
-        copies = start([
-            copy(buf.at[mine], buf.at[mine], sems, n, d) for n, d in enumerate(devices)
-        ])
-        waiting.extend(copies)
-        return copies
-
-    def summed(buf, count):
-        total = buf[0]
-        for k in range(1, count):
-            total = total + buf[k]
-        return total
-
     for n in range(2):
-        wz[z, n : n + 1] = jnp.sum(tiles[n] + folded(acc * whole[n]), axis=0, keepdims=True)
-    wz_copies = send_sums(wz, z, wz_sem, [at(z_=k) for k in zz])
+        wz[z, x, n : n + 1] = jnp.sum(tiles[n] + folded(acc * whole[n]), axis=0, keepdims=True)
+    cross = sorted(
+        ((p, q) for p in range(Z) for q in range(X) if p or q),
+        key=lambda t: -min(t[0], Z - t[0]) - min(t[1], X - t[1]),
+    )
+    wz_copies = start([
+        copy(wz.at[z, x], wz.at[z, x], wz_sem, n, at(z_=lax.rem(z + p, Z), x_=lax.rem(x + q, X)))
+        for n, (p, q) in enumerate(cross)
+    ])
+    waiting += wz_copies
     arrive(wz_copies)
-    wy[my_line] = summed(wz, Z)
-    wy_copies = send_sums(wy, my_line, wy_sem, lines)
+    sums = jnp.zeros((2, LANES), F32)
+    for k in range(Z):
+        for q in range(X):
+            sums = sums + wz[k, q]
+    wy[my_line] = sums
+    wy_copies = start([
+        copy(wy.at[my_line], wy.at[my_line], wy_sem, n, dev) for n, dev in enumerate(lines)
+    ])
+    waiting += wy_copies
     arrive(r_copies)
     cr_copies = start([copy(cr.at[core], cr.at[core], cr_sem, 0, at(c_=other))])
     waiting += cr_copies
@@ -377,10 +405,9 @@
             prior_b = (gb[1] + prior_b) * keep_01
 
     arrive(wy_copies)
-    wx[x] = summed(wy, 2 * Y)
-    wx_copies = send_sums(wx, x, wx_sem, [at(x_=k) for k in xs])
-    arrive(wx_copies)
-    total = summed(wx, X)
+    total = wy[0]
+    for k in range(1, 2 * Y):
+        total = total + wy[k]
     scale = -1.0 / (PUPIL * 2.0 * 2 * Y * Z)
     wind[0] = jnp.sum(total[0:1]) * scale
     wind[1] = jnp.sum(total[1:2]) * scale
@@ -390,23 +417,6 @@
         store.wait()
     for c in waiting:
         c.wait_send()
-
-
-def finish(field_h, sums_h, out_h, wind_h, sem):
-    frames = field_h.shape[0]
-    parts = 4
-    rows = field_h.shape[1] // parts
-    copies = [pltpu.make_async_copy(sums_h, wind_h, sem.at[0])]
-    for f in range(frames):
-        for p in range(parts):
-            here = (f, pl.ds(p * rows, rows))
-            copies.append(
-                pltpu.make_async_copy(field_h.at[here], out_h.at[here], sem.at[1 + f * parts + p])
-            )
-    for c in copies:
-        c.start()
-    for c in copies:
-        c.wait()
 
 
 def on_device(Y, Z, X, phases, focal, shifts, mask):
@@ -432,9 +442,11 @@
         V((4, BLOCK, 256), BF16),
         V((PUPIL, 256), BF16),
         V((2, FOCAL, LANES), BF16),
-        V((HALO + 32, PUPIL), BF16),
-        V((HALO + 32, PUPIL), BF16),
-        V((2 * Y, 2, LANES), jnp.int32),
+        V((HALO, PUPIL), BF16),
+        V((HALO, PUPIL), BF16),
+        V((2, PUPIL), F32),
+        V((2, PUPIL), F32),
+        V((Y, 2, 2, LANES), jnp.int32),
         V((Z, 2, LANES), jnp.int32),
         V((PUPIL, 256), BF16),
         V((X, WINDOW, 256), BF16),
@@ -455,20 +467,19 @@
         V((Y, 2, PR, LANES), F32),
         V((Y, 2, PR, LANES), F32),
         V((Y, 2, PR, LANES), F32),
-        V((Z, 2, LANES), F32),
+        V((Z, X, 2, LANES), F32),
         V((2 * Y, 2, LANES), F32),
-        V((X, 2, LANES), F32),
         V((2, BLOCK, PUPIL), F32),
         pltpu.SemaphoreType.DMA((6,)),
         pltpu.SemaphoreType.DMA((2,)),
-        sems(X), sems(X), sems(1), sems(2 * Y), sems(Z), sems(X), sems(2), sems(Y), sems(Z), sems(Y),
-        sems(1), sems(1), sems(Y), sems(Z), sems(2 * Y), sems(X),
+        sems(X), sems(X), sems(2), sems(2 * Y), sems(Z), sems(X), sems(2), sems(Y), sems(Z), sems(Y),
+        sems(1), sems(1), sems(Y), sems(X * Z), sems(2 * Y), sems(1), pltpu.SemaphoreType.REGULAR((2,)),
     ]
     shapes = (
         jax.ShapeDtypeStruct((2, BLOCK, PUPIL), F32),
         jax.ShapeDtypeStruct((2,), F32),
     )
-    field, sums = pl.pallas_call(
+    return pl.pallas_call(
         functools.partial(body, Y, Z, X),
         name="adjoint_sweep",
         out_shape=shapes,
@@ -479,15 +490,6 @@
             collective_id=1, has_side_effects=True, vmem_limit_bytes=63 << 20
         ),
     )(phases, focal, shifts, mask, jnp.asarray(by_pupil), jnp.asarray(by_focal))
-    return pl.pallas_call(
-        finish,
-        name="finish",
-        out_shape=shapes,
-        in_specs=[hbm, hbm],
-        out_specs=(hbm, hbm),
-        scratch_shapes=[pltpu.SemaphoreType.DMA((9,))],
-        compiler_params=pltpu.CompilerParams(vmem_limit_bytes=63 << 20),
-    )(field, sums)
 
 
 def solution(mesh):

time: 72.9 us -> 58.6 us (0.80)
  Pallas kernels: 72.1 us -> 55.4 us
  local copies, waits for them, and re-layouts: 0 us -> 2.38 us
    pallas_call x1 -> x0, Pallas kernels: 17.1 us -> none  [on_device(): pl.pallas_call(finish, name='finish', out_shape=shapes, in_specs=[hbm, hb...]
    unnamed x0 -> x4, local copies, waits for them, and re-layouts: none -> 2.38 us
where the time goes in v4:
time: 58.6 us; the launch traced here: 58.4 us
  Pallas kernels  55.4 us (95%)
  local copies, waits for them, and re-layouts  2.38 us (4%)
  between operations  0.65 us (1%)
    pallas_call x1, Pallas kernels, on_device(): pl.pallas_call(functools.partial(body, Y, Z, X), name='adjoint_sweep', ou...  55.4 us
    unnamed x4, local copies, waits for them, and re-layouts  2.38 us

profile of v4, /device:TPU:1, one launch (start us, length us, event | category | flops | bytes accessed | tf_op | source)
XLA Modules:
  0.0 58.4 jit_solution(7673424131320466701)
XLA Ops:
  0.6 55.4 %adjoint_sweep.1 = (f32[2,128,512]{2,1,0:T(8,128)}, f32[2]{0:T(128)}) custom-call(bf16[2,128,512]{2,1,0:T(8,128)(2,1)} %phases_h.1, bf16[2,2,64,256]{3,2,1,0:T(8,128)(2,1)} %focal_h.1, s32[2,2]{1,0:T(2,128)} %shifts_h.1, s32[128,512]{1,0:T(8,128)} %mask_h.1, bf16[512,512]{1,0:T(8,128)(2,1)} %constant.4.clone.by_pupil_h, ...), custom_call_target="tpu_custom_call" | custom-call | tf_op jit(solution)/shard_map/adjoint_sweep/pallas_call | solution.py:482
  56.0 0.0 copy-start
  56.0 1.9 %copy.10 = f32[2,128,512]{2,1,0:T(8,128)} copy(f32[2,128,512]{2,1,0:T(8,128)} %get-tuple-element.4) | data formatting | bytes 1048576
  57.9 0.0 copy-done
  57.9 0.5 copy.11
Async XLA Ops:
  56.0 1.9 %copy-start = (f32[2]{0:T(128)S(1)}, f32[2]{0:T(128)}, u32[]{:S(2)}) copy-start(f32[2]{0:T(128)} %get-tuple-element.5) | copy-start | bytes 28

commit v5 on v4

--- a/solution.py
+++ b/solution.py
@@ -88,20 +88,13 @@
 
     zs[...] = jnp.zeros((Z, PR, LANES), F32)
     def ring(d):
-        near_y = [at(y_=lax.rem(y + p, Y)) for p in sorted({d % Y, -d % Y})]
-        return near_y + [at(z_=lax.rem(z + p, Z)) for p in sorted({d % Z, -d % Z})]
-
-    rounds = [d for d in (1, 2) if 2 * d < max(Y, Z)]
-
-    def announce(n):
-        for dev in ring(rounds[n]):
-            pl.semaphore_signal(ring_sem.at[n], inc=1, device_id=dev, device_id_type=MESH)
-
-    def heard(n):
-        pl.semaphore_wait(ring_sem.at[n], len(ring(rounds[n])))
+        near_y = [at(y_=lax.rem(y + p, Y)) for p in sorted({d % Y, -d % Y} - {0})]
+        return near_y + [at(z_=lax.rem(z + p, Z)) for p in sorted({d % Z, -d % Z} - {0})]
+
+    relayed = max(Y, Z) > 5
 
     barrier = pltpu.get_barrier_semaphore()
-    entry = [at(x_=k) for k in xs] + ring(1) + [at(c_=other)]
+    entry = [at(x_=k) for k in xs] + ring(2) + ring(1) + [at(c_=other)]
     for dev in entry:
         pl.semaphore_signal(barrier, inc=1, device_id=dev, device_id_type=MESH)
     q_rows = FOCAL // X
@@ -132,8 +125,9 @@
     s_recv[y, core, 0:1] = jnp.full((1, LANES), a0 + a1, jnp.int32)
     s_recv[y, core, 1:2] = jnp.full((1, LANES), b0 + b1, jnp.int32)
     pl.semaphore_wait(barrier, len(entry))
-    if rounds:
-        announce(0)
+    if relayed:
+        for dev in ring(2):
+            pl.semaphore_signal(ring_sem, inc=1, device_id=dev, device_id_type=MESH)
     sc_copies = start([copy(s_recv.at[y, core], s_recv.at[y, core], sc_sem, 0, at(c_=other))])
     waiting += sc_copies
     loads[3].wait()
@@ -157,10 +151,8 @@
         copy(p_send, p_recv, h_sem, 0, above), copy(h_send, h_recv, h_sem, 1, above)
     ])
     waiting += y_copies + f_copies + h_copies
-    for n in range(len(rounds)):
-        heard(n)
-        if n + 1 < len(rounds):
-            announce(n + 1)
+    if relayed:
+        pl.semaphore_wait(ring_sem, len(ring(2)))
     arrive(sc_copies)
     s_copies = start([
         copy(s_recv.at[y], s_recv.at[y], s_sem, n, at(y_=k)) for n, k in enumerate(yy)
@@ -221,6 +213,13 @@
         diffs[f, 1, 0:BLOCK] = jnp.where(wide == PUPIL - 1, 0.0, pltpu.roll(now, PUPIL - 1, 1)) - now
         for n in range(2):
             diffs[f, n, BLOCK:WINDOW] = jnp.zeros((HALO, PUPIL), F32)
+    arrive(w_copies)
+    for f in range(2):
+        g = jnp.dot(w_recv[2 * f], by_focal[0:256], preferred_element_type=F32) + jnp.dot(
+            w_recv[2 * f + 1], by_focal[256:512], preferred_element_type=F32
+        )
+        grad[f, 0:BLOCK] = g[0:BLOCK] * live
+        grad[f, BLOCK:WINDOW] = g[BLOCK:WINDOW] * h_recv[0:HALO].astype(F32)
     arrive(t_copies)
     zero_tile = jnp.zeros((2, LANES), jnp.int32)
     beyond = zero_tile
@@ -270,6 +269,19 @@
 
     keep_01 = DECAY * keep(wide, col1, col0)
     keep_12 = DECAY * keep(wide, col2, col1)
+    for f in range(2):
+        gb[f] = shifted(grad[f], f)
+    seg = gb[0] + gb[1] * keep_01
+
+    for m_ in range(PIECES):
+        r, c = rows_cols(m_)
+        bseg[m_ % 2, m_ // 2] = seg[r, c]
+
+    c_copies = start([
+        copy(bseg.at[other], cx.at[other], c_sem, 0, at(c_=other)),
+        copy(bseg.at[core], cx.at[core], c_sem, 1, at(c_=other)),
+    ])
+    waiting += c_copies
     for n in range(2):
         d0b[n] = keep_01 * shifted(diffs[0, n], 0)
         weight = keep_12 * (shifted(diffs[1, n], 1) + d0b[n])
@@ -278,26 +290,6 @@
             qseg[m_ % 2, m_ // 2, n] = weight[r, c]
     qx_copies = start([copy(qseg.at[other], qx, qx_sem, 0, at(c_=other))])
     waiting += qx_copies
-
-    arrive(w_copies)
-    for f in range(2):
-        g = jnp.dot(w_recv[2 * f], by_focal[0:256], preferred_element_type=F32) + jnp.dot(
-            w_recv[2 * f + 1], by_focal[256:512], preferred_element_type=F32
-        )
-        grad[f, 0:BLOCK] = g[0:BLOCK] * live
-        grad[f, BLOCK:WINDOW] = g[BLOCK:WINDOW] * h_recv[0:HALO].astype(F32)
-        gb[f] = shifted(grad[f], f)
-    seg = gb[0] + gb[1] * keep_01
-
-    for m_ in range(PIECES):
-        r, c = rows_cols(m_)
-        bseg[m_ % 2, m_ // 2] = seg[r, c]
-
-    c_copies = start([
-        copy(bseg.at[other], cx.at[other], c_sem, 0, at(c_=other)),
-        copy(bseg.at[core], cx.at[core], c_sem, 1, at(c_=other)),
-    ])
-    waiting += c_copies
     arrive(c_copies[0:1])
     first = core == 0
     for k in range(Y):
@@ -417,6 +409,29 @@
         store.wait()
     for c in waiting:
         c.wait_send()
+
+
+def finish(field_h, sums, out_h, wind, held, sem_in, sem_out):
+    parts = sem_in.shape[0] // field_h.shape[0]
+    rows = field_h.shape[1] // parts
+    places = [(f, pl.ds(p * rows, rows)) for f in range(field_h.shape[0]) for p in range(parts)]
+    loads = [
+        pltpu.make_async_copy(field_h.at[here], held.at[here], sem_in.at[n])
+        for n, here in enumerate(places)
+    ]
+    stores = [
+        pltpu.make_async_copy(held.at[here], out_h.at[here], sem_out.at[n])
+        for n, here in enumerate(places)
+    ]
+    for load in loads:
+        load.start()
+    wind[0] = sums[0]
+    wind[1] = sums[1]
+    for load, store in zip(loads, stores):
+        load.wait()
+        store.start()
+    for store in stores:
+        store.wait()
 
 
 def on_device(Y, Z, X, phases, focal, shifts, mask):
@@ -473,13 +488,13 @@
         pltpu.SemaphoreType.DMA((6,)),
         pltpu.SemaphoreType.DMA((2,)),
         sems(X), sems(X), sems(2), sems(2 * Y), sems(Z), sems(X), sems(2), sems(Y), sems(Z), sems(Y),
-        sems(1), sems(1), sems(Y), sems(X * Z), sems(2 * Y), sems(1), pltpu.SemaphoreType.REGULAR((2,)),
+        sems(1), sems(1), sems(Y), sems(X * Z), sems(2 * Y), sems(1), pltpu.SemaphoreType.REGULAR,
     ]
     shapes = (
         jax.ShapeDtypeStruct((2, BLOCK, PUPIL), F32),
         jax.ShapeDtypeStruct((2,), F32),
     )
-    return pl.pallas_call(
+    field, sums = pl.pallas_call(
         functools.partial(body, Y, Z, X),
         name="adjoint_sweep",
         out_shape=shapes,
@@ -490,6 +505,19 @@
             collective_id=1, has_side_effects=True, vmem_limit_bytes=63 << 20
         ),
     )(phases, focal, shifts, mask, jnp.asarray(by_pupil), jnp.asarray(by_focal))
+    return pl.pallas_call(
+        finish,
+        name="finish",
+        out_shape=shapes,
+        in_specs=[hbm, smem],
+        out_specs=(hbm, smem),
+        scratch_shapes=[
+            V((2, BLOCK, PUPIL), F32),
+            pltpu.SemaphoreType.DMA((4,)),
+            pltpu.SemaphoreType.DMA((4,)),
+        ],
+        compiler_params=pltpu.CompilerParams(vmem_limit_bytes=63 << 20),
+    )(field, sums)
 
 
 def solution(mesh):

time: 58.6 us -> 58.9 us (level)
  Pallas kernels: 55.4 us -> 58.1 us
  local copies, waits for them, and re-layouts: 2.38 us -> 0 us
    pallas_call x0 -> x1, Pallas kernels: none -> 3 us  [on_device(): pl.pallas_call(finish, name='finish', out_shape=shapes, in_specs=[hbm, sm...]
    unnamed x4 -> x0, local copies, waits for them, and re-layouts: 2.38 us -> none
where the time goes in v5:
time: 58.9 us; the launch traced here: 58.8 us
  Pallas kernels  58.1 us (99%)
  between operations  0.64 us (1%)
    pallas_call x1, Pallas kernels, on_device(): pl.pallas_call(functools.partial(body, Y, Z, X), name='adjoint_sweep', ou...  55.1 us
    pallas_call x1, Pallas kernels, on_device(): pl.pallas_call(finish, name='finish', out_shape=shapes, in_specs=[hbm, sm...  3 us

profile of v5, /device:TPU:1, one launch (start us, length us, event | category | flops | bytes accessed | tf_op | source)
XLA Modules:
  0.0 58.8 jit_solution(2480829603049076624)
XLA Ops:
  0.6 55.1 %adjoint_sweep.1 = (f32[2,128,512]{2,1,0:T(8,128)}, f32[2]{0:T(128)}) custom-call(bf16[2,128,512]{2,1,0:T(8,128)(2,1)} %phases_h.1, bf16[2,2,64,256]{3,2,1,0:T(8,128)(2,1)} %focal_h.1, s32[2,2]{1,0:T(2,128)} %shifts_h.1, s32[128,512]{1,0:T(8,128)} %mask_h.1, bf16[512,512]{1,0:T(8,128)(2,1)} %constant.4.clone.by_pupil_h, ...), custom_call_target="tpu_custom_call" | custom-call | tf_op jit(solution)/shard_map/adjoint_sweep/pallas_call | solution.py:497
  55.8 3.0 %finish.1 = (f32[2,128,512]{2,1,0:T(8,128)}, f32[2]{0:T(128)}) custom-call(f32[2,128,512]{2,1,0:T(8,128)} %get-tuple-element.4.field_h, f32[2]{0:T(128)} %get-tuple-element.5.sums), custom_call_target="tpu_custom_call" | custom-call | tf_op jit(solution)/shard_map/finish/pallas_call | solution.py:508

commit v6 on v5

--- a/solution.py
+++ b/solution.py
@@ -36,7 +36,7 @@
     Y, Z, X, phases_h, focal_h, shifts_h, mask_h, by_pupil_h, by_focal_h, out_h, wind,
     phases, shifts, mask, by_pupil, by_focal,
     y_send, y_recv, f_recv, h_send, h_recv, p_send, p_recv, s_recv, t_recv, resid, w_buf, w_recv,
-    grad, gb, bseg, cx, ag, ys, zs, ret, cr, carry, diffs, d0b, qseg, qx, qc, qy, wz, wy, out,
+    grad, gb, bseg, cx, ag, ys, zs, ret, cr, carry, wide_ph, d0b, qseg, qx, qc, qy, wz, wy, out,
     in_sem, out_sem, y_sem, f_sem, h_sem, s_sem, t_sem, w_sem, c_sem, ys_sem, zs_sem, r_sem, cr_sem,
     qx_sem, qy_sem, wz_sem, wy_sem, sc_sem, ring_sem,
 ):
@@ -207,12 +207,9 @@
     arrive(h_copies)
     inner = jnp.where(x < X - 1, 1.0, 0.0).astype(F32)
     for f in range(2):
-        now = phases[f].astype(F32)
-        below = p_recv[f : f + 1] * inner
-        diffs[f, 0, 0:BLOCK] = jnp.concatenate([now[1:], below], axis=0) - now
-        diffs[f, 1, 0:BLOCK] = jnp.where(wide == PUPIL - 1, 0.0, pltpu.roll(now, PUPIL - 1, 1)) - now
-        for n in range(2):
-            diffs[f, n, BLOCK:WINDOW] = jnp.zeros((HALO, PUPIL), F32)
+        wide_ph[f, 0:BLOCK] = phases[f].astype(F32)
+        wide_ph[f, BLOCK:WINDOW] = jnp.zeros((HALO, PUPIL), F32)
+        wide_ph[f, BLOCK : BLOCK + 1] = p_recv[f : f + 1] * inner
     arrive(w_copies)
     for f in range(2):
         g = jnp.dot(w_recv[2 * f], by_focal[0:256], preferred_element_type=F32) + jnp.dot(
@@ -282,9 +279,19 @@
         copy(bseg.at[core], cx.at[core], c_sem, 1, at(c_=other)),
     ])
     waiting += c_copies
+    row_at = lax.broadcasted_iota(jnp.int32, (WINDOW, 1), 0)
+    steps = []
+    for f in range(2):
+        placed = shifted(wide_ph[f], f)
+        row = row_at - (row0, row1)[f]
+        inside = jnp.where((row >= 0) & (row < BLOCK), 1.0, 0.0).astype(F32)
+        last = wide == ((PUPIL - 1 + (col0, col1)[f]) & (PUPIL - 1))
+        down = (pltpu.roll(placed, WINDOW - 1, 0) - placed) * inside
+        side = (jnp.where(last, 0.0, pltpu.roll(placed, PUPIL - 1, 1)) - placed) * inside
+        steps.append((down, side))
     for n in range(2):
-        d0b[n] = keep_01 * shifted(diffs[0, n], 0)
-        weight = keep_12 * (shifted(diffs[1, n], 1) + d0b[n])
+        d0b[n] = keep_01 * steps[0][n]
+        weight = keep_12 * (steps[1][n] + d0b[n])
         for m_ in range(PIECES):
             r, c = rows_cols(m_)
             qseg[m_ % 2, m_ // 2, n] = weight[r, c]
@@ -411,29 +418,6 @@
         c.wait_send()
 
 
-def finish(field_h, sums, out_h, wind, held, sem_in, sem_out):
-    parts = sem_in.shape[0] // field_h.shape[0]
-    rows = field_h.shape[1] // parts
-    places = [(f, pl.ds(p * rows, rows)) for f in range(field_h.shape[0]) for p in range(parts)]
-    loads = [
-        pltpu.make_async_copy(field_h.at[here], held.at[here], sem_in.at[n])
-        for n, here in enumerate(places)
-    ]
-    stores = [
-        pltpu.make_async_copy(held.at[here], out_h.at[here], sem_out.at[n])
-        for n, here in enumerate(places)
-    ]
-    for load in loads:
-        load.start()
-    wind[0] = sums[0]
-    wind[1] = sums[1]
-    for load, store in zip(loads, stores):
-        load.wait()
-        store.start()
-    for store in stores:
-        store.wait()
-
-
 def on_device(Y, Z, X, phases, focal, shifts, mask):
     BLOCK = PUPIL // X
     WINDOW = BLOCK + HALO
@@ -476,7 +460,7 @@
         V((Y, PR16, LANES), BF16),
         V((2, Y, PR16, LANES), BF16),
         V((WINDOW, PUPIL), F32),
-        V((2, 2, WINDOW, PUPIL), F32),
+        V((2, WINDOW, PUPIL), F32),
         V((2, WINDOW, PUPIL), F32),
         V((2, Y, 2, PR, LANES), F32),
         V((Y, 2, PR, LANES), F32),
@@ -494,7 +478,7 @@
         jax.ShapeDtypeStruct((2, BLOCK, PUPIL), F32),
         jax.ShapeDtypeStruct((2,), F32),
     )
-    field, sums = pl.pallas_call(
+    return pl.pallas_call(
         functools.partial(body, Y, Z, X),
         name="adjoint_sweep",
         out_shape=shapes,
@@ -505,19 +489,6 @@
             collective_id=1, has_side_effects=True, vmem_limit_bytes=63 << 20
         ),
     )(phases, focal, shifts, mask, jnp.asarray(by_pupil), jnp.asarray(by_focal))
-    return pl.pallas_call(
-        finish,
-        name="finish",
-        out_shape=shapes,
-        in_specs=[hbm, smem],
-        out_specs=(hbm, smem),
-        scratch_shapes=[
-            V((2, BLOCK, PUPIL), F32),
-            pltpu.SemaphoreType.DMA((4,)),
-            pltpu.SemaphoreType.DMA((4,)),
-        ],
-        compiler_params=pltpu.CompilerParams(vmem_limit_bytes=63 << 20),
-    )(field, sums)
 
 
 def solution(mesh):

time: 58.9 us -> 58.2 us (0.988)
  Pallas kernels: 58.1 us -> 55 us
  local copies, waits for them, and re-layouts: 0 us -> 2.38 us
    pallas_call x1 -> x0, Pallas kernels: 3 us -> none  [on_device(): pl.pallas_call(finish, name='finish', out_shape=shapes, in_specs=[hbm, sm...]
    unnamed x0 -> x4, local copies, waits for them, and re-layouts: none -> 2.38 us
where the time goes in v6:
time: 58.2 us; the launch traced here: 58 us
  Pallas kernels  55 us (95%)
  local copies, waits for them, and re-layouts  2.38 us (4%)
  between operations  0.65 us (1%)
    pallas_call x1, Pallas kernels, on_device(): pl.pallas_call(functools.partial(body, Y, Z, X), name='adjoint_sweep', ou...  55 us
    unnamed x4, local copies, waits for them, and re-layouts  2.38 us

profile of v6, /device:TPU:1, one launch (start us, length us, event | category | flops | bytes accessed | tf_op | source)
XLA Modules:
  0.0 58.0 jit_solution(5024308398595386517)
XLA Ops:
  0.6 55.0 %adjoint_sweep.1 = (f32[2,128,512]{2,1,0:T(8,128)}, f32[2]{0:T(128)}) custom-call(bf16[2,128,512]{2,1,0:T(8,128)(2,1)} %phases_h.1, bf16[2,2,64,256]{3,2,1,0:T(8,128)(2,1)} %focal_h.1, s32[2,2]{1,0:T(2,128)} %shifts_h.1, s32[128,512]{1,0:T(8,128)} %mask_h.1, bf16[512,512]{1,0:T(8,128)(2,1)} %constant.4.clone.by_pupil_h, ...), custom_call_target="tpu_custom_call" | custom-call | tf_op jit(solution)/shard_map/adjoint_sweep/pallas_call | solution.py:481
  55.6 0.0 copy-start
  55.6 1.9 %copy.10 = f32[2,128,512]{2,1,0:T(8,128)} copy(f32[2,128,512]{2,1,0:T(8,128)} %get-tuple-element.4) | data formatting | bytes 1048576
  57.5 0.0 copy-done
  57.5 0.5 copy.11
Async XLA Ops:
  55.6 1.9 %copy-start = (f32[2]{0:T(128)S(1)}, f32[2]{0:T(128)}, u32[]{:S(2)}) copy-start(f32[2]{0:T(128)} %get-tuple-element.5) | copy-start | bytes 28

commit v7 on v6

--- a/solution.py
+++ b/solution.py
@@ -146,11 +146,7 @@
         copy(focal_h.at[k // 2, :, :, cols_of(k)], f_recv.at[:, q_of(x), :], f_sem, n, at(x_=k))
         for n, k in enumerate(xs)
     ])
-    above = at(x_=lax.rem(x + X - 1, X))
-    h_copies = start([
-        copy(p_send, p_recv, h_sem, 0, above), copy(h_send, h_recv, h_sem, 1, above)
-    ])
-    waiting += y_copies + f_copies + h_copies
+    waiting += y_copies + f_copies
     if relayed:
         pl.semaphore_wait(ring_sem, len(ring(2)))
     arrive(sc_copies)
@@ -165,6 +161,11 @@
         ret[:, PR:PR16] = jnp.zeros((Y, PR16 - PR, LANES), BF16)
 
     arrive(y_copies)
+    above = at(x_=lax.rem(x + X - 1, X))
+    h_copies = start([
+        copy(p_send, p_recv, h_sem, 0, above), copy(h_send, h_recv, h_sem, 1, above)
+    ])
+    waiting += h_copies
     loads[4].wait()
     m = jnp.dot(by_focal[...], y_recv[...], preferred_element_type=F32)
     loads[5].wait()
@@ -274,10 +275,7 @@
         r, c = rows_cols(m_)
         bseg[m_ % 2, m_ // 2] = seg[r, c]
 
-    c_copies = start([
-        copy(bseg.at[other], cx.at[other], c_sem, 0, at(c_=other)),
-        copy(bseg.at[core], cx.at[core], c_sem, 1, at(c_=other)),
-    ])
+    c_copies = start([copy(bseg.at[other], cx.at[other], c_sem, 0, at(c_=other))])
     waiting += c_copies
     row_at = lax.broadcasted_iota(jnp.int32, (WINDOW, 1), 0)
     steps = []
@@ -297,7 +295,7 @@
             qseg[m_ % 2, m_ // 2, n] = weight[r, c]
     qx_copies = start([copy(qseg.at[other], qx, qx_sem, 0, at(c_=other))])
     waiting += qx_copies
-    arrive(c_copies[0:1])
+    arrive(c_copies)
     first = core == 0
     for k in range(Y):
         mine, theirs = bseg[core, k], cx[core, k]
@@ -325,6 +323,8 @@
     ])
     waiting += qy_copies
     qy[y] = qc[y]
+    rest_copies = start([copy(bseg.at[core], cx.at[core], c_sem, 1, at(c_=other))])
+    waiting += rest_copies
     arrive(ys_copies)
     my_cols = block_cols(my_line)
     later = [None] * Y
@@ -382,7 +382,7 @@
     arrive(r_copies)
     cr_copies = start([copy(cr.at[core], cr.at[core], cr_sem, 0, at(c_=other))])
     waiting += cr_copies
-    arrive(c_copies[1:2])
+    arrive(rest_copies)
     arrive(cr_copies)
     for m_ in range(PIECES):
         r, c = rows_cols(m_)

time: 58.2 us -> 58 us (level)
  no operation moved by 1% of the time
where the time goes in v7:
time: 58 us; the launch traced here: 57.9 us
  Pallas kernels  54.9 us (95%)
  local copies, waits for them, and re-layouts  2.38 us (4%)
  between operations  0.65 us (1%)
    pallas_call x1, Pallas kernels, on_device(): pl.pallas_call(functools.partial(body, Y, Z, X), name='adjoint_sweep', ou...  54.9 us
    unnamed x4, local copies, waits for them, and re-layouts  2.38 us

profile of v7, /device:TPU:1, one launch (start us, length us, event | category | flops | bytes accessed | tf_op | source)
XLA Modules:
  0.0 57.9 jit_solution(13120006723917219908)
XLA Ops:
  0.6 54.9 %adjoint_sweep.1 = (f32[2,128,512]{2,1,0:T(8,128)}, f32[2]{0:T(128)}) custom-call(bf16[2,128,512]{2,1,0:T(8,128)(2,1)} %phases_h.1, bf16[2,2,64,256]{3,2,1,0:T(8,128)(2,1)} %focal_h.1, s32[2,2]{1,0:T(2,128)} %shifts_h.1, s32[128,512]{1,0:T(8,128)} %mask_h.1, bf16[512,512]{1,0:T(8,128)(2,1)} %constant.4.clone.by_pupil_h, ...), custom_call_target="tpu_custom_call" | custom-call | tf_op jit(solution)/shard_map/adjoint_sweep/pallas_call | solution.py:481
  55.5 0.0 copy-start
  55.5 1.9 %copy.10 = f32[2,128,512]{2,1,0:T(8,128)} copy(f32[2,128,512]{2,1,0:T(8,128)} %get-tuple-element.4) | data formatting | bytes 1048576
  57.4 0.0 copy-done
  57.4 0.5 copy.11
Async XLA Ops:
  55.5 1.9 %copy-start = (f32[2]{0:T(128)S(1)}, f32[2]{0:T(128)}, u32[]{:S(2)}) copy-start(f32[2]{0:T(128)} %get-tuple-element.5) | copy-start | bytes 28

commit v8 on v7

--- a/solution.py
+++ b/solution.py
@@ -350,14 +350,6 @@
     for k in reversed(range(1, Z)):
         new = zs[k] + acc * (DECAY ** (4 * Y) * keep(my_cols, z_cols[k + 1], z_cols[k]))
         acc = jnp.where(k > z, new, acc)
-    for k in range(Y):
-        ret[k, 0:PR] = (later[k] + acc * reach[k]).astype(BF16)
-    r_copies = start([
-        copy(ret.at[k], cr.at[core, y], r_sem, n, at(y_=k)) for n, k in enumerate(yy)
-    ])
-    waiting += r_copies
-    cr[core, y] = ret[y]
-
     for n in range(2):
         wz[z, x, n : n + 1] = jnp.sum(tiles[n] + folded(acc * whole[n]), axis=0, keepdims=True)
     cross = sorted(
@@ -369,6 +361,14 @@
         for n, (p, q) in enumerate(cross)
     ])
     waiting += wz_copies
+    for k in range(Y):
+        ret[k, 0:PR] = (later[k] + acc * reach[k]).astype(BF16)
+    r_copies = start([
+        copy(ret.at[k], cr.at[core, y], r_sem, n, at(y_=k)) for n, k in enumerate(yy)
+    ])
+    waiting += r_copies
+    cr[core, y] = ret[y]
+
     arrive(wz_copies)
     sums = jnp.zeros((2, LANES), F32)
     for k in range(Z):

time: 58 us -> 58 us (level)
  no operation moved by 1% of the time
where the time goes in v8:
time: 58 us; the launch traced here: 57.8 us
  Pallas kernels  54.8 us (94%)
  local copies, waits for them, and re-layouts  2.38 us (4%)
  between operations  0.65 us (1%)
    pallas_call x1, Pallas kernels, on_device(): pl.pallas_call(functools.partial(body, Y, Z, X), name='adjoint_sweep', ou...  54.8 us
    unnamed x4, local copies, waits for them, and re-layouts  2.38 us

profile of v8, /device:TPU:1, one launch (start us, length us, event | category | flops | bytes accessed | tf_op | source)
XLA Modules:
  0.0 57.8 jit_solution(10645481507254176908)
XLA Ops:
  0.6 54.8 %adjoint_sweep.1 = (f32[2,128,512]{2,1,0:T(8,128)}, f32[2]{0:T(128)}) custom-call(bf16[2,128,512]{2,1,0:T(8,128)(2,1)} %phases_h.1, bf16[2,2,64,256]{3,2,1,0:T(8,128)(2,1)} %focal_h.1, s32[2,2]{1,0:T(2,128)} %shifts_h.1, s32[128,512]{1,0:T(8,128)} %mask_h.1, bf16[512,512]{1,0:T(8,128)(2,1)} %constant.4.clone.by_pupil_h, ...), custom_call_target="tpu_custom_call" | custom-call | tf_op jit(solution)/shard_map/adjoint_sweep/pallas_call | solution.py:481
  55.4 0.0 copy-start
  55.4 1.9 %copy.10 = f32[2,128,512]{2,1,0:T(8,128)} copy(f32[2,128,512]{2,1,0:T(8,128)} %get-tuple-element.4) | data formatting | bytes 1048576
  57.3 0.0 copy-done
  57.3 0.5 copy.11
Async XLA Ops:
  55.4 1.9 %copy-start = (f32[2]{0:T(128)S(1)}, f32[2]{0:T(128)}, u32[]{:S(2)}) copy-start(f32[2]{0:T(128)} %get-tuple-element.5) | copy-start | bytes 28
